TPU v7x, 128 devices: a whole 4x4x4 slice. The times are simulated.
128 devices in a mesh: group: 8 (over x, core), member: 16 (over y, z).
Axes of the slice: x: 4, y: 4, z: 4, core: 2. Of those that a mesh axis runs over, the one named last changes fastest.
Arguments:
- embeddings: bfloat16 [98304, 1024], P(('group', 'member')), may hold values from -6 to 6
- labels: int32 [98304], P(('group', 'member')), may hold values from 0 to 7
- send_list: int32 [128, 768], P(('group', 'member')), may hold values from 0 to 767, each once within a row
Outputs:
- row_max: float32 [98304], P(('group', 'member'))
Inputs may be any that keep to these rules, and one draw needn't show every extreme that they name: Each row of send_list names each of the 768 local rows once.
All inputs are finite; a program needn't handle non-finite values.
Results may differ from a plain program's by a relative error of at most 0.0014.
Values may be sent and summed in bfloat16 or wider, within the bound.
No kernel may reach another device: no remote copies, remote signals or barrier semaphores. Data moves between devices by JAX's collectives and lax.ppermute only.
A program may use at most 128 MiB of HBM per device.

v0:
```python
import jax
import jax.numpy as jnp
from jax import lax
from jax.sharding import PartitionSpec as P


def shortened(array):
    return jax.tree.map(lambda a: a.astype(jnp.bfloat16) if a.dtype == jnp.float32 else a, array)


def normalize(embeddings):
    values = embeddings.astype(jnp.float32)
    scale = lax.rsqrt(jnp.sum(values * values, axis=1, keepdims=True) + 1e-06)
    return (values * scale).astype(jnp.bfloat16)


def block_scores(queries, key_rows):
    return lax.dot_general(
        queries, key_rows, (((1,), (1,)), ((), ())), preferred_element_type=jnp.float32
    )


def earlier_max(queries, q_label, q_order, key_rows, key_label, key_order):
    scores = block_scores(queries, key_rows)
    allowed = (q_label[:, None] == key_label[None, :]) & (key_order[None, :] < q_order[:, None])
    return jnp.max(jnp.where(allowed, scores, jnp.float32(-1.0)), axis=1)


def body(embeddings, labels, send_list):
    row_count, feat_width = embeddings.shape
    n_group = lax.axis_size("group")
    n_member = lax.axis_size("member")
    dev_count = n_group * n_member
    slot_rows = row_count // dev_count
    unit_rows = normalize(embeddings)
    device = lax.axis_index("group") * n_member + lax.axis_index("member")
    chosen = send_list[0]
    sent_unit = unit_rows[chosen]
    sent_label = labels[chosen]
    sent_order = device * row_count + chosen
    arrived = (
        lax.all_to_all(
            sent_unit.reshape(dev_count, slot_rows, feat_width),
            ("group", "member"),
            split_axis=0,
            concat_axis=0,
            tiled=True,
        ),
        lax.all_to_all(
            sent_label.reshape(dev_count, slot_rows),
            ("group", "member"),
            split_axis=0,
            concat_axis=0,
            tiled=True,
        ),
        lax.all_to_all(
            sent_order.reshape(dev_count, slot_rows),
            ("group", "member"),
            split_axis=0,
            concat_axis=0,
            tiled=True,
        ),
    )
    mine_unit = arrived[0].reshape(row_count, feat_width)
    mine_label = arrived[1].reshape(row_count)
    mine_order = arrived[2].reshape(row_count)
    found = earlier_max(
        mine_unit,
        mine_label,
        mine_order,
        lax.all_gather(mine_unit, "member", axis=0, tiled=True),
        lax.all_gather(mine_label, "member", axis=0, tiled=True),
        lax.all_gather(shortened(mine_order), "member", axis=0, tiled=True),
    )
    return jnp.maximum(jnp.full((row_count,), -1.0, jnp.float32), found)


def solution(mesh):
    in_specs = (P(("group", "member"), None), P(("group", "member")), P(("group", "member"), None))
    out_specs = P(("group", "member"))
    return jax.shard_map(body, mesh=mesh, in_specs=in_specs, out_specs=out_specs, check_vma=False)
```

profile of v0, /device:TPU:1, one launch (start us, length us, event | category | flops | bytes accessed | tf_op | source)
XLA Modules:
  0.0 247.4 jit_solution(6922236133298402638)
XLA Ops:
  6.5 1.8 fusion
  8.3 0.7 fusion.2
  9.1 1.7 fusion.1
  10.8 3.6 %gather_fusion.1 = bf16[768,1024]{1,0:T(8,128)(2,1)} fusion(bf16[768,1024]{1,0:T(8,128)(2,1)S(1)} %fusion.1, s32[1024]{0:T(1024)S(1)} %pad_clamp_fusion), kind=kCustom, calls=%fused_computation.1 | custom fusion | bytes 3148800 | tf_op jit(solution)/shard_map/gather | solution.py:38
  14.4 2.5 %reshape.73 = bf16[128,6,1024]{2,1,0:T(8,128)(2,1)S(1)} reshape(bf16[768,1024]{1,0:T(8,128)(2,1)} %gather_fusion.1) | data formatting | bytes 3145728 | tf_op jit(solution)/shard_map/reshape | solution.py:43
  16.9 40.9 %all_to_all.20 = bf16[128,6,1024]{2,1,0:T(8,128)(2,1)} all-to-all(bf16[128,6,1024]{2,1,0:T(8,128)(2,1)S(1)} %reshape.73), channel_id=1, replica_groups=mesh['group'=8,'member'=16] {'group','member'}, dimensions={0} | all-to-all | bytes 3145728 | tf_op jit(solution)/shard_map/all_to_all | solution.py:42
  57.8 3.7 %reshape.74 = bf16[768,1024]{1,0:T(8,128)(2,1)} reshape(bf16[128,6,1024]{2,1,0:T(8,128)(2,1)} %all_to_all.20) | data formatting | bytes 3145728 | tf_op jit(solution)/shard_map/reshape | solution.py:64
  61.5 3.2 %gather_fusion = s32[768]{0:T(1024)S(1)} fusion(s32[768]{0:T(1024)S(1)} %copy-done, s32[1024]{0:T(1024)S(1)} %pad_clamp_fusion), kind=kCustom, calls=%fused_computation | custom fusion | bytes 9216 | tf_op jit(solution)/shard_map/gather | solution.py:39
  64.7 0.8 all_to_all.13
  65.5 4.9 %all-to-all-start = ((s32[128,1,6]{2,1,0:T(1,128)}), s32[128,1,6]{2,1,0:T(1,128)S(1)}, u32[]{:S(2)}, u32[]{:S(2)}) async-start(s32[128,1,6]{2,1,0:T(1,128)} %bitcast.1), calls=%async_computation | async-start | bytes 131072 | tf_op jit(solution)/shard_map/all_to_all | solution.py:49
  70.5 0.8 add.46
  71.2 8.8 %all-to-all-done = s32[128,1,6]{2,1,0:T(1,128)S(1)} async-done(((s32[128,1,6]{2,1,0:T(1,128)}), s32[128,1,6]{2,1,0:T(1,128)S(1)}, u32[]{:S(2)}, u32[]{:S(2)}) %all-to-all-start) | async-done | bytes 3104 | tf_op jit(solution)/shard_map/all_to_all | solution.py:49
  80.0 4.5 %all-to-all-start.1 = ((s32[128,1,6]{2,1,0:T(1,128)}), s32[128,1,6]{2,1,0:T(1,128)S(1)}, u32[]{:S(2)}, u32[]{:S(2)}) async-start(s32[128,1,6]{2,1,0:T(1,128)} %bitcast.3), calls=%async_computation.1 | async-start | bytes 131072 | tf_op jit(solution)/shard_map/all_to_all | solution.py:56
  84.5 0.1 reshape.91
  84.6 9.4 %all-to-all-done.1 = s32[128,1,6]{2,1,0:T(1,128)S(1)} async-done(((s32[128,1,6]{2,1,0:T(1,128)}), s32[128,1,6]{2,1,0:T(1,128)S(1)}, u32[]{:S(2)}, u32[]{:S(2)}) %all-to-all-start.1) | async-done | bytes 3104 | tf_op jit(solution)/shard_map/all_to_all | solution.py:56
  94.2 0.5 broadcast.59
  94.7 0.8 reduce.14
  95.5 0.1 reshape.93
  95.7 0.8 reduce.15
  96.6 16.9 %all-gather = s32[16,1,768]{2,1,0:T(1,128)S(1)} all-gather(s32[1,1,768]{2,1,0:T(1,128)S(1)} %reshape.91), channel_id=1, replica_groups=mesh['group'=8,'member'=16] {'member'}, dimensions={0}, use_global_device_ids=true | all-gather | bytes 52224 | tf_op jit(solution)/shard_map/all_gather | solution.py:72
  113.6 19.3 %all-gather.1 = s32[16,1,768]{2,1,0:T(1,128)S(1)} all-gather(s32[1,1,768]{2,1,0:T(1,128)S(1)} %reshape.93), channel_id=1, replica_groups=mesh['group'=8,'member'=16] {'member'}, dimensions={0}, use_global_device_ids=true | all-gather | bytes 52224 | tf_op jit(solution)/shard_map/all_gather | solution.py:73
  132.8 81.9 %all-gather.4.cloned.1.call-done = bf16[12288,1024]{1,0:T(8,128)(2,1)} async-done(((bf16[768,1024]{1,0:T(8,128)(2,1)}), bf16[12288,1024]{1,0:T(8,128)(2,1)}) %all-gather.4.cloned.1.call-update) | async-done | bytes 25165840 | tf_op jit(solution)/shard_map/all_gather | solution.py:71
  214.7 25.2 %select_reduce_fusion = f32[768]{0:T(1024)S(1)} fusion(bf16[768,1024]{1,0:T(8,128)(2,1)S(1)} %copy-done.1, bf16[12288,1024]{1,0:T(8,128)(2,1)} %all-gather.4.cloned.1.call-done, s32[12288]{0:T(1024)S(1)} %bitcast.13, s32[12288]{0:T(1024)S(1)} %bitcast.12, s32[768]{0:T(1024)S(1)} %reshape.72, s32[768]{0:T(1024)S(1)} %eq.15), kind=kOutput, calls=%fused_computation.2 | convolution fusion | flops 19374538752 | bytes 26846208 | tf_op jit(solution)/shard_map/dot_general | solution.py:18
  239.9 0.6 broadcast_maximum_fusion
  (13 shorter events, 0.3 us)
Async XLA Ops:
  6.5 55.0 %copy-start = (s32[768]{0:T(1024)S(1)}, s32[768]{0:T(1024)}, u32[]{:S(2)}) copy-start(s32[768]{0:T(1024)} %param.4) | copy-start | bytes 9220
  6.5 208.2 %all-gather.4.cloned.1.call-start = ((), (), s32[]{:S(2)}) async-start(), calls=%async_computation.3 | async-start | bytes 26738688 | tf_op jit(solution)/shard_map/all_gather | solution.py:71
  61.5 8.9 %copy-start.2 = (s32[1,768]{1,0:T(1,128)S(1)}, s32[1,768]{1,0:T(1,128)}, u32[]{:S(2)}) copy-start(s32[1,768]{1,0:T(1,128)} %param.5) | copy-start | bytes 9220
  61.5 153.2 %copy-start.1 = (bf16[768,1024]{1,0:T(8,128)(2,1)S(1)}, bf16[768,1024]{1,0:T(8,128)(2,1)}, u32[]{:S(2)}) copy-start(bf16[768,1024]{1,0:T(8,128)(2,1)} %reshape.74) | copy-start | bytes 4718596
  65.5 14.5 %all-to-all-start = ((s32[128,1,6]{2,1,0:T(1,128)}), s32[128,1,6]{2,1,0:T(1,128)S(1)}, u32[]{:S(2)}, u32[]{:S(2)}) async-start(s32[128,1,6]{2,1,0:T(1,128)} %bitcast.1), calls=%async_computation | async-start | bytes 131072 | tf_op jit(solution)/shard_map/all_to_all | solution.py:49
  80.0 14.1 %all-to-all-start.1 = ((s32[128,1,6]{2,1,0:T(1,128)}), s32[128,1,6]{2,1,0:T(1,128)S(1)}, u32[]{:S(2)}, u32[]{:S(2)}) async-start(s32[128,1,6]{2,1,0:T(1,128)} %bitcast.3), calls=%async_computation.1 | async-start | bytes 131072 | tf_op jit(solution)/shard_map/all_to_all | solution.py:56
Sparse Core Ops, SparseCore 0:
  61.7 153.0 all-gather.3
where the time goes:
time: 248 us; the launch traced here: 247 us
  waiting for transfers between devices  100 us (40%)
  blocking collectives  77.1 us (31%)
  matrix products  25.2 us (10%)
  local copies, waits for them, and re-layouts  15.5 us (6%)
  between operations  13.5 us (5%)
  starting transfers between devices  9.42 us (4%)
  other arithmetic  6.46 us (3%)
    all_gather x1, waiting for transfers between devices, body(): lax.all_gather(mine_unit, 'member', axis=0, tiled=True)  81.9 us
    all_to_all x1, blocking collectives, body(): lax.all_to_all(sent_unit.reshape(dev_count, slot_rows, feat_width), ('gro...  40.9 us
    dot_general x1, matrix products, block_scores(): lax.dot_general(queries, key_rows, (((1,), (1,)), ((), ())), preferred_el...  25.2 us
    all_gather x1, blocking collectives, body(): lax.all_gather(shortened(mine_order), 'member', axis=0, tiled=True)  19.3 us
    all_gather x1, blocking collectives, body(): lax.all_gather(mine_label, 'member', axis=0, tiled=True)  16.9 us
    all_to_all x1, waiting for transfers between devices, body(): lax.all_to_all(sent_order.reshape(dev_count, slot_rows), ('group', 'membe...  9.42 us
    all_to_all x1, waiting for transfers between devices, body(): lax.all_to_all(sent_label.reshape(dev_count, slot_rows), ('group', 'membe...  8.78 us
  transfers between devices with their start and end apart: 3, of which 3 were waited for; matrix products, arithmetic and copies ran while one was open for 3% of the time, Pallas kernels for 0%

commit v1 on v0

v1 whole, which is shorter than its diff:
```python
import functools

import jax
import jax.numpy as jnp
from jax import lax
from jax.experimental import pallas as pl
from jax.experimental.pallas import tpu as pltpu
from jax.sharding import Mesh, PartitionSpec as P

F32 = jnp.float32
BF = jnp.bfloat16
I32 = jnp.int32

D = 1024
ROWS = 768
CHIPS = 64
LABELS = 8
CAP = 15
SLOT = 16
MAIN = CHIPS * SLOT
FIX = LABELS * SLOT
ALL = ("x", "core", "yh", "yl", "z")
CHIP_AXES = ("x", "yh", "yl", "z")
GROUP_CHIPS = ("yl", "z")
PLANE = ("core", "yh", "yl", "z")
NEVER = 1.0e9
VMEM = 48 * 1024 * 1024


def iota(shape, dim):
    return lax.broadcasted_iota(I32, shape, dim)


def onehot(cond):
    return jnp.where(cond, 1.0, 0.0).astype(BF)


def mm(a, b):
    return lax.dot_general(a, b, (((1,), (0,)), ((), ())), preferred_element_type=F32)


def mm_t(a, b):
    return lax.dot_general(a, b, (((1,), (1,)), ((), ())), preferred_element_type=F32)


def pack_kernel(ids_ref, emb_ref, lab_ref, list_ref, out_ref):
    rot = ids_ref[2]
    listed = onehot(iota((ROWS, ROWS), 0) == list_ref[...])
    pos = iota((16, ROWS), 1)
    group_of = lax.shift_right_logical(pos * 683, 16)
    sel = iota((16, ROWS), 0)
    vals = jnp.where(sel == 0, group_of, jnp.where(sel == 1, pos - group_of * 96, 0)).astype(F32).astype(BF)
    gd = mm_t(vals, listed)
    group = gd[0:1]
    dest = gd[1:2]
    label = lab_ref[...].astype(F32)
    cluster = group * 8.0 + label
    member = iota((CHIPS, ROWS), 0).astype(F32) == cluster
    before = onehot(iota((ROWS, ROWS), 0) < iota((ROWS, ROWS), 1))
    ranks = mm(onehot(member), before)
    rank = jnp.sum(jnp.where(member, ranks, 0.0), axis=0, keepdims=True)
    count = jnp.broadcast_to(jnp.sum(jnp.where(member, 1.0, 0.0), axis=1, keepdims=True), (CHIPS, 128))
    over = jnp.maximum(count - CAP, 0.0).astype(BF)
    free = jnp.maximum(CAP - count, 0.0)
    c0, c1 = iota((CHIPS, CHIPS), 0), iota((CHIPS, CHIPS), 1)
    same = lax.shift_right_logical(c0, 3) == lax.shift_right_logical(c1, 3)
    over_pre = mm(onehot(same & (c1 < c0)), over)
    above = (CAP - 1 - (iota((CHIPS, 128), 1) & 15)).astype(F32)
    higher = jnp.clip(free, 0.0, jnp.maximum(above, 0.0)).astype(BF)
    level = onehot(free > above)
    free_pre = mm(onehot(same), higher) + mm(onehot(same & (((c1 - rot) & 7) < ((c0 - rot) & 7))), level)
    over_at = jnp.sum(jnp.where(member, over_pre[:, 0:1], 0.0), axis=0, keepdims=True) + rank - CAP
    row_code = jnp.where(rank < CAP, cluster * 16.0 + rank, 2048.0 + group * 128.0 + over_at)
    slot = iota((MAIN, 128), 0)
    at = (slot & 15).astype(F32)
    chip_hot = onehot(lax.shift_right_logical(iota((MAIN, CHIPS), 0), 4) == iota((MAIN, CHIPS), 1))
    slot_count = mm(chip_hot, count.astype(BF))
    slot_free = jnp.where(iota((MAIN, 128), 1) == (slot & 15), mm(chip_hot, free_pre.astype(BF)), 0.0)
    slot_free = jnp.sum(slot_free, axis=1, keepdims=True)
    spare = 2048.0 + (lax.shift_right_logical(slot, 7) * 128).astype(F32) + slot_free
    slot_code = jnp.where(at >= CAP, -1.0, jnp.where(at < slot_count, slot.astype(F32), spare))
    pick = jnp.concatenate([onehot(slot_code == row_code[:, b * 128:(b + 1) * 128]) for b in range(ROWS // 128)], axis=1)
    values = emb_ref[...].astype(F32)
    scale = lax.rsqrt(jnp.sum(values * values, axis=1, keepdims=True) + 1e-06)
    unit = (values * scale).astype(BF)
    lane = iota((128, ROWS), 0)
    tags = jnp.where(lane < 16, label + 1.0, jnp.where(lane < 32, dest, 0.0)).astype(BF)
    tag = jnp.where((iota((MAIN, 128), 1) & 15) == (slot & 15), mm_t(pick, tags), 0.0)
    tag = jnp.broadcast_to(jnp.sum(tag.reshape(CHIPS, SLOT, 128), axis=1, keepdims=True), (CHIPS, SLOT, 128)).reshape(MAIN, 128)
    for b in range(0, D, 256):
        part = mm(pick, unit[:, b:b + 256])
        if b == 0:
            out_ref[:, 0:128] = jnp.where(at >= CAP, tag, part[:, 0:128]).astype(BF)
            out_ref[:, 128:256] = part[:, 128:256].astype(BF)
        else:
            out_ref[:, b:b + 256] = part.astype(BF)


def tag_rows(first, n):
    pick = onehot(iota((n, n * SLOT), 1) == iota((n, n * SLOT), 0) * SLOT + CAP)
    return mm(pick, first).astype(BF)


def tag_lanes(tags, n, k):
    spread = onehot(iota((128, n * SLOT), 0) == (iota((128, n * SLOT), 1) & 15) + 16 * k)
    wide = mm(tags, spread)
    own = iota((n, n * SLOT), 0) == lax.shift_right_logical(iota((n, n * SLOT), 1), 4)
    return jnp.sum(jnp.where(own, wide, 0.0), axis=0, keepdims=True)


def tag_columns(tags, n, ks):
    spread = onehot(lax.shift_right_logical(iota((n * SLOT, n), 0), 4) == iota((n * SLOT, n), 1))
    wide = mm(spread, tags)
    shape = (n * SLOT, 128)
    own = iota(shape, 0) & 15
    return [jnp.sum(jnp.where(iota(shape, 1) == own + 16 * k, wide, 0.0), axis=1, keepdims=True) for k in ks]


def source_of(chip, core):
    return lax.shift_right_logical(chip, 4) * 32 + core * 16 + (chip & 15)


def main_order(shape, dim, core):
    slot = iota(shape, dim)
    return (source_of(lax.shift_right_logical(slot, 4), core) * 256 + (slot & 15)).astype(F32)


def away_order(source, turn, at):
    return (source * 256 + 16 + (CAP - 1 - at) * 8 + turn).astype(F32)


def fix_order(shape, dim, core, chip, at):
    holder = lax.shift_right_logical(iota(shape, dim), 4)
    chip = chip.astype(I32)
    return away_order(source_of(chip, core), (holder - chip) & 7, at.astype(I32))


def fix_kernel(ids_ref, main_ref, out_ref, flag_ref):
    own = ids_ref[1].astype(F32)
    tags = tag_rows(main_ref[:, 0:128], CHIPS)
    label = tag_lanes(tags, CHIPS, 0)
    dest = tag_lanes(tags, CHIPS, 1)
    moved = (label > 0.5) & (label != own + 1.0)
    member = moved & (iota((LABELS, MAIN), 0).astype(F32) == label - 1.0)
    before = onehot(iota((MAIN, MAIN), 0) < iota((MAIN, MAIN), 1))
    hot = jnp.concatenate([jnp.where(member, 1.0, 0.0), jnp.zeros((LABELS, MAIN), F32)], axis=0).astype(BF)
    ranks = mm(hot, before)[0:LABELS]
    rank = jnp.sum(jnp.where(member, ranks, 0.0), axis=0, keepdims=True)
    code = jnp.where(moved & (rank < CAP), (label - 1.0) * 16.0 + rank, -1.0)
    pick = onehot(iota((FIX, MAIN), 0).astype(F32) == code)
    slot = iota((1, MAIN), 1)
    lane = iota((128, MAIN), 0)
    kind = lax.shift_right_logical(lane, 4)
    vals = jnp.where(kind == 0, 1.0, jnp.where(kind == 1, lax.shift_right_logical(slot, 4).astype(F32), jnp.where(kind == 2, (slot & 15).astype(F32), jnp.where(kind == 3, dest, 0.0)))).astype(BF)
    fixed = (FIX, 128)
    tag = jnp.where((iota(fixed, 1) & 15) == (iota(fixed, 0) & 15), mm_t(pick, vals), 0.0)
    tag = jnp.broadcast_to(jnp.sum(tag.reshape(LABELS, SLOT, 128), axis=1, keepdims=True), (LABELS, SLOT, 128)).reshape(fixed)
    for b in range(0, D, 256):
        part = mm(pick, main_ref[:, b:b + 256])
        if b == 0:
            out_ref[:, 0:128] = jnp.where((iota(fixed, 0) & 15) == CAP, tag, part[:, 0:128]).astype(BF)
            out_ref[:, 128:256] = part[:, 128:256].astype(BF)
        else:
            out_ref[:, b:b + 256] = part.astype(BF)
    worst = jnp.max(jnp.where(moved, rank, 0.0), axis=1, keepdims=True)
    flag_ref[...] = jnp.broadcast_to(jnp.where(worst >= CAP, 1.0, 0.0), (8, 128))


def lanes_to_rows(row):
    return jnp.concatenate([row[:, i * 128:(i + 1) * 128] for i in range(row.shape[1] // 128)], axis=0)


def score_kernel(ids_ref, flag_ref, own_ref, twin_ref, fix_ref, fix_twin_ref, out_ref):
    core = ids_ref[0]
    mine = ids_ref[1].astype(F32) + 1.0
    tags = tag_rows(own_ref[:, 0:128], CHIPS)
    twin_tags = tag_rows(twin_ref[:, 0:128], CHIPS)
    fix_tags = tag_rows(fix_ref[:, 0:128], LABELS)
    fix_twin_tags = tag_rows(fix_twin_ref[:, 0:128], LABELS)

    def main_key(t, c):
        (label,) = tag_columns(t, CHIPS, (0,))
        return jnp.where(label == mine, main_order((MAIN, 1), 0, c), NEVER)

    def fix_key(t, c):
        valid, chip, at = tag_columns(t, LABELS, (0, 1, 2))
        return jnp.where(valid > 0.5, fix_order((FIX, 1), 0, c, chip, at), NEVER)

    keys = (
        (own_ref, main_key(tags, core)),
        (twin_ref, main_key(twin_tags, 1 - core)),
        (fix_ref, fix_key(fix_tags, core)),
        (fix_twin_ref, fix_key(fix_twin_tags, 1 - core)),
    )
    valid = tag_lanes(tags, CHIPS, 0) == mine
    query = jnp.where(valid, main_order((1, MAIN), 1, core), -1.0)
    code = jnp.where(valid, tag_lanes(tags, CHIPS, 1), -1.0)
    fix_valid = tag_lanes(fix_tags, LABELS, 0) > 0.5
    fix_chip = tag_lanes(fix_tags, LABELS, 1)
    fix_query = jnp.where(fix_valid, fix_order((1, FIX), 1, core, fix_chip, tag_lanes(fix_tags, LABELS, 2)), -1.0)
    fix_source = source_of(fix_chip.astype(I32), core).astype(F32)
    fix_code = jnp.where(fix_valid, fix_source * 128.0 + tag_lanes(fix_tags, LABELS, 3), -1.0)

    def best(q_rows, q_order, limits):
        found = jnp.full((1, q_rows.shape[0]), -1.0, F32)
        for (ref, order), limit in zip(keys, limits):
            for k in range(0, limit, 256):
                e = min(k + 256, limit)
                scores = mm_t(ref[k:e, :], q_rows)
                scores = jnp.where(order[k:e] < q_order, scores, -1.0)
                found = jnp.maximum(found, jnp.max(scores, axis=0, keepdims=True))
        return found

    rows = []
    for q in range(0, MAIN, 256):
        rows.append(lanes_to_rows(best(own_ref[q:q + 256, :], query[:, q:q + 256], (q + 256, q + 256, FIX, FIX))))
    found = jnp.concatenate(rows, axis=0)
    fix_found = best(fix_ref[...], fix_query, (MAIN, MAIN, FIX, FIX))
    table = jnp.concatenate([found, lanes_to_rows(code), fix_found, fix_code, flag_ref[0:1, :], jnp.zeros((5, 128), F32)], axis=0)
    for i in range(32):
        out_ref[i] = table


def split3(v):
    a = v.astype(BF)
    r = v - a.astype(F32)
    b = r.astype(BF)
    return a, b, (r - b.astype(F32)).astype(BF)


def place_kernel(ids_ref, in_ref, out_ref, flag_ref):
    core = ids_ref[0]
    base = (ids_ref[3] * 6).astype(F32)
    wide = (128, 128)
    outs = []
    spread = [onehot(iota(wide, 1) == lax.shift_right_logical(iota(wide, 0), 4) * 6 + q) for q in range(6)]
    fix_val, fix_code = [], []
    for c in range(2):
        acc = [jnp.zeros((8, 128), F32) for _ in range(6)]
        for k in range(LABELS):
            dev = c * 16 + core * 8 + k
            val = in_ref[dev, 0:8, :]
            code = in_ref[dev, 8:16, :]
            for q in range(6):
                acc[q] = acc[q] + jnp.where(code == base + q, val, 0.0)
            fix_val.append(in_ref[dev, 16:17, :])
            fix_code.append(in_ref[dev, 17:18, :])
        total = jnp.zeros((8, 128), F32)
        for q in range(6):
            for part in split3(acc[q]):
                total = total + mm(part, spread[q])
        outs.append(total)
    main = jnp.concatenate([outs[c][2 * x:2 * x + 2] for x in range(4) for c in range(2)], axis=0)
    val = jnp.concatenate(fix_val, axis=1)
    code = jnp.concatenate(fix_code, axis=1).astype(I32)
    source = lax.shift_right_arithmetic(code, 7)
    q = (code & 127).astype(F32) - base
    ok = (code >= 0) & (q >= 0.0) & (q < 6.0)
    n = val.shape[1]
    left = jnp.where(ok & (iota((16, n), 0) == lax.shift_right_arithmetic(source, 3)), val, 0.0)
    right = onehot(iota((128, n), 0).astype(F32) == (source & 7).astype(F32) * 6.0 + q)
    for part in split3(left):
        main = main + mm_t(part, right)
    out_ref[...] = jnp.maximum(main, -1.0)
    flag = in_ref[0, 16:24, :]
    for i in range(1, 32):
        flag = jnp.maximum(flag, in_ref[i, 16:24, :])
    flag_ref[...] = flag


def call(kernel, shapes, args, flops):
    specs = [pl.BlockSpec(memory_space=pltpu.SMEM)] + [pl.BlockSpec(memory_space=pltpu.VMEM)] * (len(args) - 1)
    return pl.pallas_call(
        kernel,
        out_shape=shapes,
        in_specs=specs,
        out_specs=jax.tree.map(lambda _: pl.BlockSpec(memory_space=pltpu.VMEM), shapes),
        compiler_params=pltpu.CompilerParams(vmem_limit_bytes=VMEM),
        cost_estimate=pl.CostEstimate(flops=flops, bytes_accessed=4 << 20, transcendentals=0),
    )(*args)


def struct(shape, dtype):
    return jax.ShapeDtypeStruct(shape, dtype)


def place(table, ids):
    back = lax.all_to_all(table, PLANE, split_axis=0, concat_axis=0, tiled=True)
    out, flag = call(place_kernel, (struct((16, 128), F32), struct((8, 128), F32)), (ids, back), 1 << 27)
    return out[:, :48].reshape(ROWS), flag


def general_path(main, ids, label_of_chip, core):
    tags = main.reshape(CHIPS, SLOT, D)[:, CAP, :32].astype(F32)
    label = tags[:, 0:16].reshape(MAIN)
    dest = tags[:, 16:32].reshape(MAIN)
    slot = jnp.arange(MAIN, dtype=I32)
    chip = slot // 16
    home = main_order((MAIN,), 0, core)
    away = away_order(source_of(chip, core), (label_of_chip - chip) & 7, slot & 15)
    order = jnp.where(label == (label_of_chip + 1).astype(F32), home, away)
    key_order = jnp.where(label > 0.5, order, NEVER)
    axes = ("core", "yl", "z")
    ring = [(i, (i + 1) % 16) for i in range(16)]

    def step(_, state):
        found, rows, tag = state
        scores = mm_t(main, rows)
        ok = (tag[0:1] == label[:, None]) & (tag[1:2] < order[:, None])
        found = jnp.maximum(found, jnp.max(jnp.where(ok, scores, -1.0), axis=1))
        return found, lax.ppermute(rows, axes, ring), lax.ppermute(tag, axes, ring)

    tag = jnp.stack([label, key_order])
    found, _, _ = lax.fori_loop(0, 16, step, (jnp.full((MAIN,), -1.0, F32), main, tag))
    code = jnp.where(label > 0.5, dest, -1.0)
    none = jnp.full((8, 128), -1.0, F32)
    table = jnp.concatenate([found.reshape(8, 128), code.reshape(8, 128), none], axis=0)
    out, _ = place(jnp.broadcast_to(table, (32, 24, 128)), ids)
    return out


def body(embeddings, labels, send_list):
    core = lax.axis_index("core").astype(I32)
    member = lax.axis_index(("yh", "yl", "z")).astype(I32)
    label_of_chip = member & 7
    ids = jnp.stack([core, label_of_chip, label_of_chip, member])
    packed = call(
        pack_kernel, struct((MAIN, D), BF), (ids, embeddings, labels.reshape(1, ROWS), send_list), 3 << 30
    )
    main = lax.all_to_all(
        packed.reshape(CHIPS, SLOT, D), CHIP_AXES, split_axis=0, concat_axis=0, tiled=True
    ).reshape(MAIN, D)
    swap = [(0, 1), (1, 0)]
    twin = lax.ppermute(main, "core", swap)
    fix, flag = call(fix_kernel, (struct((FIX, D), BF), struct((8, 128), F32)), (ids, main), 1 << 30)
    fix = lax.all_to_all(
        fix.reshape(LABELS, SLOT, D), GROUP_CHIPS, split_axis=0, concat_axis=0, tiled=True
    ).reshape(FIX, D)
    fix_twin = lax.ppermute(fix, "core", swap)
    table = call(score_kernel, struct((32, 24, 128), F32), (ids, flag, main, twin, fix, fix_twin), 4 << 30)
    out, flag = place(table, ids)
    return lax.cond(
        jnp.max(flag[2, 0]) > 0.0,
        lambda: general_path(main, ids, label_of_chip, core),
        lambda: out,
    )


def solution(mesh):
    fine = Mesh(mesh.devices.reshape(4, 2, 2, 2, 4), ALL)
    return jax.shard_map(body, mesh=fine, in_specs=(P(ALL, None), P(ALL), P(ALL, None)), out_specs=P(ALL), check_vma=False)
```

time: 248 us -> 87.3 us (0.35)
  waiting for transfers between devices: 100 us -> 10.8 us
  blocking collectives: 77.1 us -> 48.5 us
  matrix products: 25.2 us -> 0 us
  Pallas kernels: 0 us -> 14.5 us
  between operations: 13.5 us -> 0.7 us
  local copies, waits for them, and re-layouts: 15.5 us -> 3.98 us
  other arithmetic: 6.46 us -> 0.08 us
    all_gather x1 -> x0, waiting for transfers between devices: 81.9 us -> none  [body(): lax.all_gather(mine_unit, 'member', axis=0, tiled=True)]
    all_gather x2 -> x0, blocking collectives: 36.2 us -> none  [the longest x1 19.3 us: body(): lax.all_gather(shortened(mine_order), 'member', axis=0, tiled=True)]
    dot_general x1 -> x0, matrix products: 25.2 us -> none  [block_scores(): lax.dot_general(queries, key_rows, (((1,), (1,)), ((), ())), preferred_el...]
    pallas_call x0 -> x4, Pallas kernels: none -> 14.5 us  [call(): pl.pallas_call(kernel, out_shape=shapes, in_specs=specs, out_specs=jax.tr...]
    all_to_all x2 -> x1, waiting for transfers between devices: 18.2 us -> 9.65 us  [place(): back = lax.all_to_all(table, PLANE, split_axis=0, concat_axis=0, tiled=True)]
    all_to_all x1 -> x2, blocking collectives: 40.9 us -> 48.5 us  [the longest x1 39.4 us: body(): lax.all_to_all(packed.reshape(CHIPS, SLOT, D), CHIP_AXES, split_axis=0, c...]
    gather x2 -> x0, local copies, waits for them, and re-layouts: 6.76 us -> none  [the longest x1 3.58 us: body(): sent_unit = unit_rows[chosen]]
    reshape x3 -> x2, local copies, waits for them, and re-layouts: 6.35 us -> 0.76 us  [the longest x1 0.69 us: body(): labels.reshape(1, ROWS)]
  transfers between devices with their start and end apart: 3 -> 3, of which waited for: 3 -> 2; matrix products, arithmetic and copies ran while one was open for 3% -> 0% of each run, Pallas kernels for 0% -> 2%
where the time goes in v1:
time: 87.3 us; the launch traced here: 87 us
  blocking collectives  48.5 us (56%)
  Pallas kernels  14.5 us (17%)
  waiting for transfers between devices  10.8 us (12%)
  starting transfers between devices  8.22 us (9%)
  local copies, waits for them, and re-layouts  3.98 us (5%)
    all_to_all x1, blocking collectives, body(): lax.all_to_all(packed.reshape(CHIPS, SLOT, D), CHIP_AXES, split_axis=0, c...  39.4 us
    pallas_call x4, Pallas kernels, call(): pl.pallas_call(kernel, out_shape=shapes, in_specs=specs, out_specs=jax.tr...  14.5 us
    all_to_all x1, waiting for transfers between devices, place(): back = lax.all_to_all(table, PLANE, split_axis=0, concat_axis=0, tiled=True)  9.65 us
    all_to_all x1, blocking collectives, body(): lax.all_to_all(fix.reshape(LABELS, SLOT, D), GROUP_CHIPS, split_axis=0, c...  9.1 us
    all_to_all x1, starting transfers between devices, place(): back = lax.all_to_all(table, PLANE, split_axis=0, concat_axis=0, tiled=True)  4.01 us
    ppermute x1, starting transfers between devices, body(): twin = lax.ppermute(main, 'core', swap)  2.99 us
    unnamed x6, local copies, waits for them, and re-layouts  2.68 us
  transfers between devices with their start and end apart: 3, of which 2 were waited for; matrix products, arithmetic and copies ran while one was open for 0% of the time, Pallas kernels for 2%

profile of v1, /device:TPU:1, one launch (start us, length us, event | category | flops | bytes accessed | tf_op | source)
XLA Modules:
  0.0 87.0 jit_solution(6639279758281629710)
XLA Ops:
  0.0 0.7 reshape.176.lab_ref
  0.7 0.1 pad_add_fusion.ids_ref
  0.8 0.0 copy-start
  0.8 1.4 %copy-done = bf16[768,1024]{1,0:T(8,128)(2,1)S(1)} copy-done((bf16[768,1024]{1,0:T(8,128)(2,1)S(1)}, bf16[768,1024]{1,0:T(8,128)(2,1)}, u32[]{:S(2)}) %copy-start) | copy-done | bytes 1572888
  2.2 0.0 copy-start.1
  2.2 0.7 copy-done.1
  2.9 4.3 %shard_map.39 = bf16[1024,1024]{1,0:T(8,128)(2,1)S(1)} custom-call(s32[4]{0:T(128)S(1)} %pad_add_fusion.ids_ref, bf16[768,1024]{1,0:T(8,128)(2,1)S(1)} %copy-done, s32[1,768]{1,0:T(1,128)S(1)} %reshape.176.lab_ref, s32[1,768]{1,0:T(1,128)S(1)} %copy-done.1), custom_call_target="tpu_custom_call" | custom-call | flops 3221225472 | bytes 4194304 | tf_op jit(solution)/shard_map/pallas_call | solution.py:273
  7.2 39.4 %all_to_all.20 = bf16[64,16,1024]{2,1,0:T(8,128)(2,1)S(1)} all-to-all(bf16[64,16,1024]{2,1,0:T(8,128)(2,1)S(1)} %bitcast.32), channel_id=1, replica_groups=mesh['x'=4,'core'=2,'yh'=2,'yl'=2,'z'=4] {'x','yh','yl','z'}, dimensions={0} | all-to-all | bytes 4194304 | tf_op jit(solution)/shard_map/all_to_all | solution.py:330
  46.6 3.0 %collective-permute-start.2 = (bf16[1024,1024]{1,0:T(8,128)(2,1)S(1)}, bf16[1024,1024]{1,0:T(8,128)(2,1)S(1)}, u32[]{:S(2)}, u32[]{:S(2)}) collective-permute-start(bf16[1024,1024]{1,0:T(8,128)(2,1)S(1)} %bitcast.37), channel_id=1, source_target_pairs={{0,16},{16,0},{1,17},{17,1},{2,18},{18,2},{3,19},{19,3},{4,20},{20... | collective-permute-start | bytes 6291464 | tf_op jit(solution)/shard_map/ppermute | solution.py:334
  49.6 1.6 %shard_map.40 = (bf16[128,1024]{1,0:T(8,128)(2,1)S(1)}, f32[8,128]{1,0:T(8,128)S(1)}) custom-call(s32[4]{0:T(128)S(1)} %pad_add_fusion.ids_ref, bf16[1024,1024]{1,0:T(8,128)(2,1)S(1)} %bitcast.38), custom_call_target="tpu_custom_call" | custom-call | flops 1073741824 | bytes 4194304 | tf_op jit(solution)/shard_map/pallas_call | solution.py:273
  51.2 9.1 %all_to_all.21 = bf16[8,16,1024]{2,1,0:T(8,128)(2,1)S(1)} all-to-all(bf16[8,16,1024]{2,1,0:T(8,128)(2,1)S(1)} %bitcast.35), channel_id=1, replica_groups=mesh['x'=4,'core'=2,'yh'=2,'yl'=2,'z'=4] {'yl','z'}, dimensions={0} | all-to-all | bytes 524288 | tf_op jit(solution)/shard_map/all_to_all | solution.py:336
  60.3 1.2 %collective-permute-start.3 = (bf16[128,1024]{1,0:T(8,128)(2,1)S(1)}, bf16[128,1024]{1,0:T(8,128)(2,1)S(1)}, u32[]{:S(2)}, u32[]{:S(2)}) collective-permute-start(bf16[128,1024]{1,0:T(8,128)(2,1)S(1)} %bitcast.33), channel_id=1, source_target_pairs={{0,16},{16,0},{1,17},{17,1},{2,18},{18,2},{3,19},{19,3},{4,20},{20... | collective-permute-start | bytes 786440 | tf_op jit(solution)/shard_map/ppermute | solution.py:339
  61.6 1.2 %collective-permute-done.3.fix_twin_ref = bf16[128,1024]{1,0:T(8,128)(2,1)S(1)} collective-permute-done((bf16[128,1024]{1,0:T(8,128)(2,1)S(1)}, bf16[128,1024]{1,0:T(8,128)(2,1)S(1)}, u32[]{:S(2)}, u32[]{:S(2)}) %collective-permute-start.3) | collective-permute-done | bytes 262176 | tf_op jit(solution)/shard_map/ppermute | solution.py:339
  62.7 0.0 collective-permute-done.2.twin_ref
  62.7 7.2 %shard_map.41 = f32[32,24,128]{2,1,0:T(8,128)} custom-call(s32[4]{0:T(128)S(1)} %pad_add_fusion.ids_ref, f32[8,128]{1,0:T(8,128)S(1)} %get-tuple-element.69.flag_ref, bf16[1024,1024]{1,0:T(8,128)(2,1)S(1)} %bitcast.39, bf16[1024,1024]{1,0:T(8,128)(2,1)S(1)} %collective-permute-done.2.twin_ref, bf16[128,1024]{1,0:T(8,128)(2,1)S(1)} %bitcast.34, ...), custom_call_target="tpu_custom_call" | custom-call | flops 4294967296 | bytes 4194304 | tf_op jit(solution)/shard_map/pallas_call | solution.py:273
  69.9 4.0 %all-to-all-start.3 = ((f32[32,24,128]{2,1,0:T(8,128)}), f32[32,24,128]{2,1,0:T(8,128)S(1)}, u32[]{:S(2)}, u32[]{:S(2)}) async-start(f32[32,24,128]{2,1,0:T(8,128)} %shard_map.41), calls=%async_computation.3 | async-start | bytes 786432 | tf_op jit(solution)/shard_map/all_to_all | solution.py:288
  73.9 9.6 %all-to-all-done.3.in_ref = f32[32,24,128]{2,1,0:T(8,128)S(1)} async-done(((f32[32,24,128]{2,1,0:T(8,128)}), f32[32,24,128]{2,1,0:T(8,128)S(1)}, u32[]{:S(2)}, u32[]{:S(2)}) %all-to-all-start.3) | async-done | bytes 393248 | tf_op jit(solution)/shard_map/all_to_all | solution.py:288
  83.6 1.4 %shard_map.42 = (f32[16,128]{1,0:T(8,128)S(1)}, f32[8,128]{1,0:T(8,128)S(1)}) custom-call(s32[4]{0:T(128)S(1)} %pad_add_fusion.ids_ref, f32[32,24,128]{2,1,0:T(8,128)S(1)} %all-to-all-done.3.in_ref), custom_call_target="tpu_custom_call" | custom-call | flops 134217728 | bytes 4194304 | tf_op jit(solution)/shard_map/pallas_call | solution.py:273
  84.9 0.5 slice.25
  86.1 0.3 conditional.1
  86.1 0.1 reshape.167
  86.4 0.0 copy-start.4
  86.4 0.6 copy-done.4
Async XLA Ops:
  0.8 1.4 %copy-start = (bf16[768,1024]{1,0:T(8,128)(2,1)S(1)}, bf16[768,1024]{1,0:T(8,128)(2,1)}, u32[]{:S(2)}) copy-start(bf16[768,1024]{1,0:T(8,128)(2,1)} %emb_ref.1) | copy-start | bytes 4718596
  2.2 0.7 copy-start.1
  46.6 16.1 %collective-permute-start.2 = (bf16[1024,1024]{1,0:T(8,128)(2,1)S(1)}, bf16[1024,1024]{1,0:T(8,128)(2,1)S(1)}, u32[]{:S(2)}, u32[]{:S(2)}) collective-permute-start(bf16[1024,1024]{1,0:T(8,128)(2,1)S(1)} %bitcast.37), channel_id=1, source_target_pairs={{0,16},{16,0},{1,17},{17,1},{2,18},{18,2},{3,19},{19,3},{4,20},{20... | collective-permute-start | bytes 6291464 | tf_op jit(solution)/shard_map/ppermute | solution.py:334
  60.3 2.4 %collective-permute-start.3 = (bf16[128,1024]{1,0:T(8,128)(2,1)S(1)}, bf16[128,1024]{1,0:T(8,128)(2,1)S(1)}, u32[]{:S(2)}, u32[]{:S(2)}) collective-permute-start(bf16[128,1024]{1,0:T(8,128)(2,1)S(1)} %bitcast.33), channel_id=1, source_target_pairs={{0,16},{16,0},{1,17},{17,1},{2,18},{18,2},{3,19},{19,3},{4,20},{20... | collective-permute-start | bytes 786440 | tf_op jit(solution)/shard_map/ppermute | solution.py:339
  69.9 13.7 %all-to-all-start.3 = ((f32[32,24,128]{2,1,0:T(8,128)}), f32[32,24,128]{2,1,0:T(8,128)S(1)}, u32[]{:S(2)}, u32[]{:S(2)}) async-start(f32[32,24,128]{2,1,0:T(8,128)} %shard_map.41), calls=%async_computation.3 | async-start | bytes 786432 | tf_op jit(solution)/shard_map/all_to_all | solution.py:288
  86.4 0.6 copy-start.4

commit v2 on v1

--- a/solution.py
+++ b/solution.py
@@ -43,8 +43,16 @@
     return lax.dot_general(a, b, (((1,), (1,)), ((), ())), preferred_element_type=F32)
 
 
-def pack_kernel(ids_ref, emb_ref, lab_ref, list_ref, out_ref):
+def pack_kernel(ids_ref, emb_hbm, lab_hbm, list_hbm, out_hbm, emb_ref, lab_ref, list_ref, out_ref, sems, out_sems):
+    copies = [
+        pltpu.make_async_copy(src, dst, sems.at[i])
+        for i, (src, dst) in enumerate(((list_hbm, list_ref), (lab_hbm, lab_ref), (emb_hbm, emb_ref)))
+    ]
+    for copy in copies:
+        copy.start()
     rot = ids_ref[2]
+    copies[0].wait()
+    copies[1].wait()
     listed = onehot(iota((ROWS, ROWS), 0) == list_ref[...])
     pos = iota((16, ROWS), 1)
     group_of = lax.shift_right_logical(pos * 683, 16)
@@ -53,7 +61,7 @@
     gd = mm_t(vals, listed)
     group = gd[0:1]
     dest = gd[1:2]
-    label = lab_ref[...].astype(F32)
+    label = lab_ref[...].reshape(1, ROWS).astype(F32)
     cluster = group * 8.0 + label
     member = iota((CHIPS, ROWS), 0).astype(F32) == cluster
     before = onehot(iota((ROWS, ROWS), 0) < iota((ROWS, ROWS), 1))
@@ -80,6 +88,7 @@
     spare = 2048.0 + (lax.shift_right_logical(slot, 7) * 128).astype(F32) + slot_free
     slot_code = jnp.where(at >= CAP, -1.0, jnp.where(at < slot_count, slot.astype(F32), spare))
     pick = jnp.concatenate([onehot(slot_code == row_code[:, b * 128:(b + 1) * 128]) for b in range(ROWS // 128)], axis=1)
+    copies[2].wait()
     values = emb_ref[...].astype(F32)
     scale = lax.rsqrt(jnp.sum(values * values, axis=1, keepdims=True) + 1e-06)
     unit = (values * scale).astype(BF)
@@ -87,13 +96,18 @@
     tags = jnp.where(lane < 16, label + 1.0, jnp.where(lane < 32, dest, 0.0)).astype(BF)
     tag = jnp.where((iota((MAIN, 128), 1) & 15) == (slot & 15), mm_t(pick, tags), 0.0)
     tag = jnp.broadcast_to(jnp.sum(tag.reshape(CHIPS, SLOT, 128), axis=1, keepdims=True), (CHIPS, SLOT, 128)).reshape(MAIN, 128)
-    for b in range(0, D, 256):
+    copies = []
+    for i, b in enumerate(range(0, D, 256)):
         part = mm(pick, unit[:, b:b + 256])
         if b == 0:
             out_ref[:, 0:128] = jnp.where(at >= CAP, tag, part[:, 0:128]).astype(BF)
             out_ref[:, 128:256] = part[:, 128:256].astype(BF)
         else:
             out_ref[:, b:b + 256] = part.astype(BF)
+        copies.append(pltpu.make_async_copy(out_ref.at[:, b:b + 256], out_hbm.at[:, b:b + 256], out_sems.at[i]))
+        copies[-1].start()
+    for copy in copies:
+        copy.wait()
 
 
 def tag_rows(first, n):
@@ -170,55 +184,84 @@
     return jnp.concatenate([row[:, i * 128:(i + 1) * 128] for i in range(row.shape[1] // 128)], axis=0)
 
 
-def score_kernel(ids_ref, flag_ref, own_ref, twin_ref, fix_ref, fix_twin_ref, out_ref):
+def best(keys, q_rows, q_order):
+    found = jnp.full((1, q_rows.shape[0]), -1.0, F32)
+    for rows, order in keys:
+        scores = jnp.where(order[:, 0:1] < q_order, mm_t(rows[...], q_rows), -1.0)
+        found = jnp.maximum(found, jnp.max(scores, axis=0, keepdims=True))
+    return found
+
+
+def main_kernel(ids_ref, own_ref, twin_ref, rows_ref, own_key_ref, twin_key_ref, code_ref):
     core = ids_ref[0]
     mine = ids_ref[1].astype(F32) + 1.0
     tags = tag_rows(own_ref[:, 0:128], CHIPS)
     twin_tags = tag_rows(twin_ref[:, 0:128], CHIPS)
+
+    def main_key(t, c):
+        (label,) = tag_columns(t, CHIPS, (0,))
+        return jnp.broadcast_to(jnp.where(label == mine, main_order((MAIN, 1), 0, c), NEVER), (MAIN, 128))
+
+    own_key_ref[...] = main_key(tags, core)
+    twin_key_ref[...] = main_key(twin_tags, 1 - core)
+    valid = tag_lanes(tags, CHIPS, 0) == mine
+    query = jnp.where(valid, main_order((1, MAIN), 1, core), -1.0)
+    dest = tag_lanes(tags, CHIPS, 1).astype(I32)
+    home = lax.shift_right_logical(dest * 43, 8)
+    member = valid & (iota((16, MAIN), 0) == home)
+    before = onehot(iota((MAIN, MAIN), 0) < iota((MAIN, MAIN), 1))
+    ranks = mm(onehot(member), before)
+    rank = jnp.sum(jnp.where(member, ranks, 0.0), axis=0, keepdims=True)
+    rank = jnp.where(valid, rank, -1.0)
+    hot = onehot(iota((128, MAIN), 0).astype(F32) == rank)
+    source = source_of(lax.shift_right_logical(iota((1, MAIN), 1), 4), core)
+    at = source * 6 + dest - home * 6 + 1
+    high = lax.shift_right_logical(at, 4)
+    parts = [jnp.where(member, part.astype(F32), 0.0).astype(BF) for part in (high, at - high * 16)]
+    code_ref[...] = mm_t(parts[0], hot) * 16.0 + mm_t(parts[1], hot) - 1.0
+    worst = jnp.max(rank, axis=1, keepdims=True)
+    found = [
+        best(
+            ((own_ref[0:q + 256, :], own_key_ref[0:q + 256, :]), (twin_ref[0:q + 256, :], twin_key_ref[0:q + 256, :])),
+            own_ref[q:q + 256, :],
+            query[:, q:q + 256],
+        )
+        for q in range(0, MAIN, 256)
+    ]
+    found = jnp.concatenate(found, axis=1)
+    worst = jnp.broadcast_to(worst, (1, MAIN))
+    rows = jnp.concatenate([query, found, home.astype(F32), worst, rank, jnp.zeros((3, MAIN), F32)], axis=0)
+    rows_ref[...] = rows
+
+
+def last_kernel(ids_ref, flag_ref, rows_ref, own_key_ref, twin_key_ref, code_ref, own_ref, twin_ref, fix_ref, fix_twin_ref, out_ref):
+    core = ids_ref[0]
     fix_tags = tag_rows(fix_ref[:, 0:128], LABELS)
     fix_twin_tags = tag_rows(fix_twin_ref[:, 0:128], LABELS)
-
-    def main_key(t, c):
-        (label,) = tag_columns(t, CHIPS, (0,))
-        return jnp.where(label == mine, main_order((MAIN, 1), 0, c), NEVER)
 
     def fix_key(t, c):
         valid, chip, at = tag_columns(t, LABELS, (0, 1, 2))
         return jnp.where(valid > 0.5, fix_order((FIX, 1), 0, c, chip, at), NEVER)
 
-    keys = (
-        (own_ref, main_key(tags, core)),
-        (twin_ref, main_key(twin_tags, 1 - core)),
-        (fix_ref, fix_key(fix_tags, core)),
-        (fix_twin_ref, fix_key(fix_twin_tags, 1 - core)),
-    )
-    valid = tag_lanes(tags, CHIPS, 0) == mine
-    query = jnp.where(valid, main_order((1, MAIN), 1, core), -1.0)
-    code = jnp.where(valid, tag_lanes(tags, CHIPS, 1), -1.0)
+    fix_rows = jnp.concatenate([fix_ref[...], fix_twin_ref[...]], axis=0)
+    fix_keys = ((fix_rows, jnp.concatenate([fix_key(fix_tags, core), fix_key(fix_twin_tags, 1 - core)], axis=0)),)
     fix_valid = tag_lanes(fix_tags, LABELS, 0) > 0.5
     fix_chip = tag_lanes(fix_tags, LABELS, 1)
     fix_query = jnp.where(fix_valid, fix_order((1, FIX), 1, core, fix_chip, tag_lanes(fix_tags, LABELS, 2)), -1.0)
     fix_source = source_of(fix_chip.astype(I32), core).astype(F32)
     fix_code = jnp.where(fix_valid, fix_source * 128.0 + tag_lanes(fix_tags, LABELS, 3), -1.0)
-
-    def best(q_rows, q_order, limits):
-        found = jnp.full((1, q_rows.shape[0]), -1.0, F32)
-        for (ref, order), limit in zip(keys, limits):
-            for k in range(0, limit, 256):
-                e = min(k + 256, limit)
-                scores = mm_t(ref[k:e, :], q_rows)
-                scores = jnp.where(order[k:e] < q_order, scores, -1.0)
-                found = jnp.maximum(found, jnp.max(scores, axis=0, keepdims=True))
-        return found
-
-    rows = []
-    for q in range(0, MAIN, 256):
-        rows.append(lanes_to_rows(best(own_ref[q:q + 256, :], query[:, q:q + 256], (q + 256, q + 256, FIX, FIX))))
-    found = jnp.concatenate(rows, axis=0)
-    fix_found = best(fix_ref[...], fix_query, (MAIN, MAIN, FIX, FIX))
-    table = jnp.concatenate([found, lanes_to_rows(code), fix_found, fix_code, flag_ref[0:1, :], jnp.zeros((5, 128), F32)], axis=0)
-    for i in range(32):
-        out_ref[i] = table
+    fix_found = best(((own_ref, own_key_ref), (twin_ref, twin_key_ref)) + fix_keys, fix_ref[...], fix_query)
+    found = jnp.maximum(best(fix_keys, own_ref[...], rows_ref[0:1, :]), rows_ref[1:2, :])
+    here = iota((16, MAIN), 0).astype(F32) == rows_ref[2:3, :]
+    value = jnp.concatenate([jnp.where(here, part.astype(F32), 0.0).astype(BF) for part in split3(found)], axis=0)
+    value = mm_t(value, onehot(iota((128, MAIN), 0).astype(F32) == rows_ref[4:5, :]))
+    value = value[0:16] + value[16:32] + value[32:48]
+    flag = jnp.maximum(flag_ref[0:1, :], jnp.where(rows_ref[3:4, 0:128] >= 128.0, 1.0, 0.0))
+    common = jnp.concatenate([fix_found, fix_code, flag, jnp.zeros((3, 128), F32)], axis=0)
+    for m in range(16):
+        table = jnp.concatenate([value[m:m + 1], code_ref[m:m + 1], common], axis=0)
+        out_ref[m] = table
+        out_ref[16 + m] = table
 
 
 def split3(v):
@@ -228,7 +271,7 @@
     return a, b, (r - b.astype(F32)).astype(BF)
 
 
-def place_kernel(ids_ref, in_ref, out_ref, flag_ref):
+def place_kernel(ids_ref, in_ref, out_ref):
     core = ids_ref[0]
     base = (ids_ref[3] * 6).astype(F32)
     wide = (128, 128)
@@ -262,20 +305,46 @@
     for part in split3(left):
         main = main + mm_t(part, right)
     out_ref[...] = jnp.maximum(main, -1.0)
-    flag = in_ref[0, 16:24, :]
+
+
+def put_kernel(ids_ref, in_ref, out_ref, flag_ref):
+    core = ids_ref[0]
+    base = ids_ref[3] * 6
+    val, at = [], []
+    for c in range(2):
+        for k in range(LABELS):
+            block = in_ref[c * 16 + core * 8 + k]
+            val.append(block[0:1])
+            at.append(block[1:2].astype(I32))
+            val.append(block[2:3])
+            code = block[3:4].astype(I32)
+            q = (code & 127) - base
+            ok = (code >= 0) & (q >= 0) & (q < 6)
+            at.append(jnp.where(ok, lax.shift_right_arithmetic(code, 7) * 6 + q, -1))
+    val = jnp.concatenate(val, axis=1)
+    at = jnp.concatenate(at, axis=1)
+    n = val.shape[1]
+    left = jnp.where(iota((8, n), 0) == lax.shift_right_arithmetic(at, 7), val, 0.0)
+    right = onehot(iota((128, n), 0) == (at & 127))
+    out = jnp.zeros((8, 128), F32)
+    for part in split3(left):
+        out = out + mm_t(part, right)
+    out_ref[...] = jnp.maximum(out, -1.0)[0:6]
+    flag = in_ref[0]
     for i in range(1, 32):
-        flag = jnp.maximum(flag, in_ref[i, 16:24, :])
+        flag = jnp.maximum(flag, in_ref[i])
     flag_ref[...] = flag
 
 
-def call(kernel, shapes, args, flops):
-    specs = [pl.BlockSpec(memory_space=pltpu.SMEM)] + [pl.BlockSpec(memory_space=pltpu.VMEM)] * (len(args) - 1)
+def call(kernel, shapes, args, flops, memory=pltpu.VMEM, scratch=(), vmem=VMEM, out_memory=pltpu.VMEM):
+    specs = [pl.BlockSpec(memory_space=pltpu.SMEM)] + [pl.BlockSpec(memory_space=memory)] * (len(args) - 1)
     return pl.pallas_call(
         kernel,
         out_shape=shapes,
         in_specs=specs,
-        out_specs=jax.tree.map(lambda _: pl.BlockSpec(memory_space=pltpu.VMEM), shapes),
-        compiler_params=pltpu.CompilerParams(vmem_limit_bytes=VMEM),
+        out_specs=jax.tree.map(lambda _: pl.BlockSpec(memory_space=out_memory), shapes),
+        scratch_shapes=scratch,
+        compiler_params=pltpu.CompilerParams(vmem_limit_bytes=vmem),
         cost_estimate=pl.CostEstimate(flops=flops, bytes_accessed=4 << 20, transcendentals=0),
     )(*args)
 
@@ -286,8 +355,8 @@
 
 def place(table, ids):
     back = lax.all_to_all(table, PLANE, split_axis=0, concat_axis=0, tiled=True)
-    out, flag = call(place_kernel, (struct((16, 128), F32), struct((8, 128), F32)), (ids, back), 1 << 27)
-    return out[:, :48].reshape(ROWS), flag
+    out = call(place_kernel, struct((16, 128), F32), (ids, back), 1 << 27)
+    return out[:, :48].reshape(ROWS)
 
 
 def general_path(main, ids, label_of_chip, core):
@@ -315,8 +384,7 @@
     code = jnp.where(label > 0.5, dest, -1.0)
     none = jnp.full((8, 128), -1.0, F32)
     table = jnp.concatenate([found.reshape(8, 128), code.reshape(8, 128), none], axis=0)
-    out, _ = place(jnp.broadcast_to(table, (32, 24, 128)), ids)
-    return out
+    return place(jnp.broadcast_to(table, (32, 24, 128)), ids)
 
 
 def body(embeddings, labels, send_list):
@@ -325,7 +393,21 @@
     label_of_chip = member & 7
     ids = jnp.stack([core, label_of_chip, label_of_chip, member])
     packed = call(
-        pack_kernel, struct((MAIN, D), BF), (ids, embeddings, labels.reshape(1, ROWS), send_list), 3 << 30
+        pack_kernel,
+        struct((MAIN, D), BF),
+        (ids, embeddings, labels, send_list),
+        3 << 30,
+        pltpu.HBM,
+        (
+            pltpu.VMEM((ROWS, D), BF),
+            pltpu.VMEM((ROWS,), I32),
+            pltpu.VMEM((1, ROWS), I32),
+            pltpu.VMEM((MAIN, D), BF),
+            pltpu.SemaphoreType.DMA((3,)),
+            pltpu.SemaphoreType.DMA((4,)),
+        ),
+        56 * 1024 * 1024,
+        pltpu.HBM,
     )
     main = lax.all_to_all(
         packed.reshape(CHIPS, SLOT, D), CHIP_AXES, split_axis=0, concat_axis=0, tiled=True
@@ -336,13 +418,18 @@
     fix = lax.all_to_all(
         fix.reshape(LABELS, SLOT, D), GROUP_CHIPS, split_axis=0, concat_axis=0, tiled=True
     ).reshape(FIX, D)
+    wide = struct((MAIN, 128), F32)
+    shapes = (struct((8, MAIN), F32), wide, wide, struct((16, 128), F32))
+    parts = call(main_kernel, shapes, (ids, main, twin), 3 << 30)
+    fix, code = lax.optimization_barrier((fix, parts[3]))
     fix_twin = lax.ppermute(fix, "core", swap)
-    table = call(score_kernel, struct((32, 24, 128), F32), (ids, flag, main, twin, fix, fix_twin), 4 << 30)
-    out, flag = place(table, ids)
+    table = call(last_kernel, struct((32, 8, 128), F32), (ids, flag, *parts[:3], code, main, twin, fix, fix_twin), 1 << 30)
+    back = lax.all_to_all(table, PLANE, split_axis=0, concat_axis=0, tiled=True)
+    out, flag = call(put_kernel, (struct((6, 128), F32), struct((8, 128), F32)), (ids, back), 1 << 27)
     return lax.cond(
-        jnp.max(flag[2, 0]) > 0.0,
+        flag[4, 0] > 0.0,
         lambda: general_path(main, ids, label_of_chip, core),
-        lambda: out,
+        lambda: out.reshape(ROWS),
     )
 
 

time: 87.3 us -> 84.4 us (0.967)
  blocking collectives: 48.5 us -> 39.8 us
  Pallas kernels: 14.5 us -> 20.9 us
  starting transfers between devices: 8.22 us -> 11.5 us
  local copies, waits for them, and re-layouts: 3.98 us -> 1.11 us
  waiting for transfers between devices: 10.8 us -> 9.85 us
    all_to_all x1 -> x0, blocking collectives: 9.1 us -> none  [body(): lax.all_to_all(fix.reshape(LABELS, SLOT, D), GROUP_CHIPS, split_axis=0, c...]
    pallas_call x4 -> x5, Pallas kernels: 14.5 us -> 20.9 us  [call(): pl.pallas_call(kernel, out_shape=shapes, in_specs=specs, out_specs=jax.tr...]
    all_to_all x1 -> x2, starting transfers between devices: 4.01 us -> 7.4 us  [the longest x1 3.99 us: body(): back = lax.all_to_all(table, PLANE, split_axis=0, concat_axis=0, tiled=True)]
    unnamed x6 -> x2, local copies, waits for them, and re-layouts: 2.68 us -> 0.59 us
    all_to_all x1 -> x2, waiting for transfers between devices: 9.65 us -> 8.69 us  [the longest x1 7.54 us: body(): back = lax.all_to_all(table, PLANE, split_axis=0, concat_axis=0, tiled=True)]
  transfers between devices with their start and end apart: 3 -> 4, of which waited for: 2 -> 3; matrix products, arithmetic and copies ran while one was open for 0% -> 0% of each run, Pallas kernels for 2% -> 11%
where the time goes in v2:
time: 84.4 us; the launch traced here: 83.9 us
  blocking collectives  39.8 us (47%)
  Pallas kernels  20.9 us (25%)
  starting transfers between devices  11.5 us (14%)
  waiting for transfers between devices  9.85 us (12%)
  local copies, waits for them, and re-layouts  1.11 us (1%)
    all_to_all x1, blocking collectives, body(): lax.all_to_all(packed.reshape(CHIPS, SLOT, D), CHIP_AXES, split_axis=0, c...  39.8 us
    pallas_call x5, Pallas kernels, call(): pl.pallas_call(kernel, out_shape=shapes, in_specs=specs, out_specs=jax.tr...  20.9 us
    all_to_all x1, waiting for transfers between devices, body(): back = lax.all_to_all(table, PLANE, split_axis=0, concat_axis=0, tiled=True)  7.54 us
    all_to_all x1, starting transfers between devices, body(): back = lax.all_to_all(table, PLANE, split_axis=0, concat_axis=0, tiled=True)  3.99 us
    all_to_all x1, starting transfers between devices, body(): lax.all_to_all(fix.reshape(LABELS, SLOT, D), GROUP_CHIPS, split_axis=0, c...  3.41 us
    ppermute x1, starting transfers between devices, body(): twin = lax.ppermute(main, 'core', swap)  2.94 us
  transfers between devices with their start and end apart: 4, of which 3 were waited for; matrix products, arithmetic and copies ran while one was open for 0% of the time, Pallas kernels for 11%

profile of v2, /device:TPU:1, one launch (start us, length us, event | category | flops | bytes accessed | tf_op | source)
XLA Modules:
  0.0 83.9 jit_solution(12155243659869194835)
XLA Ops:
  0.0 0.1 pad_add_fusion.ids_ref
  0.1 5.9 %shard_map.39 = bf16[1024,1024]{1,0:T(8,128)(2,1)} custom-call(s32[4]{0:T(128)S(1)} %pad_add_fusion.ids_ref, bf16[768,1024]{1,0:T(8,128)(2,1)} %emb_hbm.1, s32[768]{0:T(1024)} %lab_hbm.1, s32[1,768]{1,0:T(1,128)} %list_hbm.1), custom_call_target="tpu_custom_call" | custom-call | flops 3221225472 | bytes 4194304 | tf_op jit(solution)/shard_map/pallas_call | solution.py:341
  6.0 39.8 %all_to_all.20 = bf16[64,16,1024]{2,1,0:T(8,128)(2,1)} all-to-all(bf16[64,16,1024]{2,1,0:T(8,128)(2,1)} %bitcast.35), channel_id=1, replica_groups=mesh['x'=4,'core'=2,'yh'=2,'yl'=2,'z'=4] {'x','yh','yl','z'}, dimensions={0} | all-to-all | bytes 4194304 | tf_op jit(solution)/shard_map/all_to_all | solution.py:412
  45.8 2.9 %collective-permute-start.2 = (bf16[1024,1024]{1,0:T(8,128)(2,1)}, bf16[1024,1024]{1,0:T(8,128)(2,1)S(1)}, u32[]{:S(2)}, u32[]{:S(2)}) collective-permute-start(bf16[1024,1024]{1,0:T(8,128)(2,1)} %bitcast.8.main_ref.own_ref), channel_id=1, source_target_pairs={{0,16},{16,0},{1,17},{17,1},{2,18},{18,2},{3,19},{19,3},{4,20},{20... | collective-permute-start | bytes 6291464 | tf_op jit(solution)/shard_map/ppermute | solution.py:416
  48.7 3.4 %shard_map.40 = (bf16[128,1024]{1,0:T(8,128)(2,1)}, f32[8,128]{1,0:T(8,128)S(1)}) custom-call(s32[4]{0:T(128)S(1)} %pad_add_fusion.ids_ref, bf16[1024,1024]{1,0:T(8,128)(2,1)} %bitcast.8.main_ref.own_ref), custom_call_target="tpu_custom_call" | custom-call | flops 1073741824 | bytes 4194304 | tf_op jit(solution)/shard_map/pallas_call | solution.py:341
  52.1 3.4 %all-to-all-start.2 = ((bf16[8,16,1024]{2,1,0:T(8,128)(2,1)}), bf16[8,16,1024]{2,1,0:T(8,128)(2,1)S(1)}, u32[]{:S(2)}, u32[]{:S(2)}) async-start(bf16[8,16,1024]{2,1,0:T(8,128)(2,1)} %bitcast.9), calls=%async_computation.2 | async-start | bytes 524288 | tf_op jit(solution)/shard_map/all_to_all | solution.py:418
  55.5 0.0 collective-permute-done.2.twin_ref
  55.5 5.5 %shard_map.41 = (f32[8,1024]{1,0:T(8,128)S(1)}, f32[1024,128]{1,0:T(8,128)S(1)}, f32[1024,128]{1,0:T(8,128)S(1)}, f32[16,128]{1,0:T(8,128)S(1)}) custom-call(s32[4]{0:T(128)S(1)} %pad_add_fusion.ids_ref, bf16[1024,1024]{1,0:T(8,128)(2,1)} %bitcast.8.main_ref.own_ref, bf16[1024,1024]{1,0:T(8,128)(2,1)S(1)} %collective-permute-done.2.twin_ref), custom_call_target="tpu_custom_call" | custom-call | flops 3221225472 | bytes 4194304 | tf_op jit(solution)/shard_map/pallas_call | solution.py:341
  61.1 1.2 %all-to-all-done.2 = bf16[8,16,1024]{2,1,0:T(8,128)(2,1)S(1)} async-done(((bf16[8,16,1024]{2,1,0:T(8,128)(2,1)}), bf16[8,16,1024]{2,1,0:T(8,128)(2,1)S(1)}, u32[]{:S(2)}, u32[]{:S(2)}) %all-to-all-start.2) | async-done | bytes 262176 | tf_op jit(solution)/shard_map/all_to_all | solution.py:418
  62.2 1.1 %collective-permute-start.3 = (bf16[128,1024]{1,0:T(8,128)(2,1)S(1)}, bf16[128,1024]{1,0:T(8,128)(2,1)S(1)}, u32[]{:S(2)}, u32[]{:S(2)}) collective-permute-start(bf16[128,1024]{1,0:T(8,128)(2,1)S(1)} %bitcast.32), channel_id=1, source_target_pairs={{0,16},{16,0},{1,17},{17,1},{2,18},{18,2},{3,19},{19,3},{4,20},{20... | collective-permute-start | bytes 786440 | tf_op jit(solution)/shard_map/ppermute | solution.py:425
  63.4 1.2 %collective-permute-done.3.fix_twin_ref = bf16[128,1024]{1,0:T(8,128)(2,1)S(1)} collective-permute-done((bf16[128,1024]{1,0:T(8,128)(2,1)S(1)}, bf16[128,1024]{1,0:T(8,128)(2,1)S(1)}, u32[]{:S(2)}, u32[]{:S(2)}) %collective-permute-start.3) | collective-permute-done | bytes 262176 | tf_op jit(solution)/shard_map/ppermute | solution.py:425
  64.6 4.6 %shard_map.42 = f32[32,8,128]{2,1,0:T(8,128)} custom-call(s32[4]{0:T(128)S(1)} %pad_add_fusion.ids_ref, f32[8,128]{1,0:T(8,128)S(1)} %get-tuple-element.71.flag_ref, f32[8,1024]{1,0:T(8,128)S(1)} %get-tuple-element.72.rows_ref, f32[1024,128]{1,0:T(8,128)S(1)} %get-tuple-element.73.own_key_ref, f32[1024,128]{1,0:T(8,128)S(1)} %get-tuple-element.74.twin_key_ref, ...), custom_call_target="tpu_custom_call" | custom-call | flops 1073741824 | bytes 4194304 | tf_op jit(solution)/shard_map/pallas_call | solution.py:341
  69.1 4.0 %all-to-all-start.3 = ((f32[32,8,128]{2,1,0:T(8,128)}), f32[32,8,128]{2,1,0:T(8,128)S(1)}, u32[]{:S(2)}, u32[]{:S(2)}) async-start(f32[32,8,128]{2,1,0:T(8,128)} %shard_map.42), calls=%async_computation.3 | async-start | bytes 262144 | tf_op jit(solution)/shard_map/all_to_all | solution.py:427
  73.1 7.5 %all-to-all-done.3.in_ref = f32[32,8,128]{2,1,0:T(8,128)S(1)} async-done(((f32[32,8,128]{2,1,0:T(8,128)}), f32[32,8,128]{2,1,0:T(8,128)S(1)}, u32[]{:S(2)}, u32[]{:S(2)}) %all-to-all-start.3) | async-done | bytes 131104 | tf_op jit(solution)/shard_map/all_to_all | solution.py:427
  80.7 1.5 %shard_map.43 = (f32[6,128]{1,0:T(8,128)S(1)}, f32[8,128]{1,0:T(8,128)S(1)}) custom-call(s32[4]{0:T(128)S(1)} %pad_add_fusion.ids_ref, f32[32,8,128]{2,1,0:T(8,128)S(1)} %all-to-all-done.3.in_ref), custom_call_target="tpu_custom_call" | custom-call | flops 134217728 | bytes 4194304 | tf_op jit(solution)/shard_map/pallas_call | solution.py:341
  82.1 0.5 slice.21
  83.3 0.0 copy-start.1
  83.3 0.6 copy-done.1
  (1 shorter events, 0.0 us)
Async XLA Ops:
  45.8 9.7 %collective-permute-start.2 = (bf16[1024,1024]{1,0:T(8,128)(2,1)}, bf16[1024,1024]{1,0:T(8,128)(2,1)S(1)}, u32[]{:S(2)}, u32[]{:S(2)}) collective-permute-start(bf16[1024,1024]{1,0:T(8,128)(2,1)} %bitcast.8.main_ref.own_ref), channel_id=1, source_target_pairs={{0,16},{16,0},{1,17},{17,1},{2,18},{18,2},{3,19},{19,3},{4,20},{20... | collective-permute-start | bytes 6291464 | tf_op jit(solution)/shard_map/ppermute | solution.py:416
  52.1 10.1 %all-to-all-start.2 = ((bf16[8,16,1024]{2,1,0:T(8,128)(2,1)}), bf16[8,16,1024]{2,1,0:T(8,128)(2,1)S(1)}, u32[]{:S(2)}, u32[]{:S(2)}) async-start(bf16[8,16,1024]{2,1,0:T(8,128)(2,1)} %bitcast.9), calls=%async_computation.2 | async-start | bytes 524288 | tf_op jit(solution)/shard_map/all_to_all | solution.py:418
  62.2 2.3 %collective-permute-start.3 = (bf16[128,1024]{1,0:T(8,128)(2,1)S(1)}, bf16[128,1024]{1,0:T(8,128)(2,1)S(1)}, u32[]{:S(2)}, u32[]{:S(2)}) collective-permute-start(bf16[128,1024]{1,0:T(8,128)(2,1)S(1)} %bitcast.32), channel_id=1, source_target_pairs={{0,16},{16,0},{1,17},{17,1},{2,18},{18,2},{3,19},{19,3},{4,20},{20... | collective-permute-start | bytes 786440 | tf_op jit(solution)/shard_map/ppermute | solution.py:425
  69.1 11.5 %all-to-all-start.3 = ((f32[32,8,128]{2,1,0:T(8,128)}), f32[32,8,128]{2,1,0:T(8,128)S(1)}, u32[]{:S(2)}, u32[]{:S(2)}) async-start(f32[32,8,128]{2,1,0:T(8,128)} %shard_map.42), calls=%async_computation.3 | async-start | bytes 262144 | tf_op jit(solution)/shard_map/all_to_all | solution.py:427
  83.3 0.6 copy-start.1

commit v3 on v2

--- a/solution.py
+++ b/solution.py
@@ -24,7 +24,7 @@
 GROUP_CHIPS = ("yl", "z")
 PLANE = ("core", "yh", "yl", "z")
 NEVER = 1.0e9
-VMEM = 48 * 1024 * 1024
+VMEM = 24 * 1024 * 1024
 
 
 def iota(shape, dim):
@@ -41,6 +41,18 @@
 
 def mm_t(a, b):
     return lax.dot_general(a, b, (((1,), (1,)), ((), ())), preferred_element_type=F32)
+
+
+def earlier(hot):
+    n, width = hot.shape
+    parts = width // 128
+    rows = jnp.concatenate([hot[:, i * 128:(i + 1) * 128] for i in range(parts)], axis=0)
+    inside = mm(rows.astype(BF), onehot(iota((128, 128), 0) < iota((128, 128), 1)))
+    total = jnp.broadcast_to(jnp.sum(rows, axis=1, keepdims=True), rows.shape).astype(BF)
+    m = parts * n
+    a, b = iota((m, m), 0), iota((m, m), 1)
+    inside = inside + mm(onehot(((a & (n - 1)) == (b & (n - 1))) & (b < a)), total)
+    return jnp.concatenate([inside[i * n:(i + 1) * n] for i in range(parts)], axis=1)
 
 
 def pack_kernel(ids_ref, emb_hbm, lab_hbm, list_hbm, out_hbm, emb_ref, lab_ref, list_ref, out_ref, sems, out_sems):
@@ -64,8 +76,7 @@
     label = lab_ref[...].reshape(1, ROWS).astype(F32)
     cluster = group * 8.0 + label
     member = iota((CHIPS, ROWS), 0).astype(F32) == cluster
-    before = onehot(iota((ROWS, ROWS), 0) < iota((ROWS, ROWS), 1))
-    ranks = mm(onehot(member), before)
+    ranks = earlier(jnp.where(member, 1.0, 0.0))
     rank = jnp.sum(jnp.where(member, ranks, 0.0), axis=0, keepdims=True)
     count = jnp.broadcast_to(jnp.sum(jnp.where(member, 1.0, 0.0), axis=1, keepdims=True), (CHIPS, 128))
     over = jnp.maximum(count - CAP, 0.0).astype(BF)
@@ -156,9 +167,7 @@
     dest = tag_lanes(tags, CHIPS, 1)
     moved = (label > 0.5) & (label != own + 1.0)
     member = moved & (iota((LABELS, MAIN), 0).astype(F32) == label - 1.0)
-    before = onehot(iota((MAIN, MAIN), 0) < iota((MAIN, MAIN), 1))
-    hot = jnp.concatenate([jnp.where(member, 1.0, 0.0), jnp.zeros((LABELS, MAIN), F32)], axis=0).astype(BF)
-    ranks = mm(hot, before)[0:LABELS]
+    ranks = earlier(jnp.where(member, 1.0, 0.0))
     rank = jnp.sum(jnp.where(member, ranks, 0.0), axis=0, keepdims=True)
     code = jnp.where(moved & (rank < CAP), (label - 1.0) * 16.0 + rank, -1.0)
     pick = onehot(iota((FIX, MAIN), 0).astype(F32) == code)
@@ -192,7 +201,9 @@
     return found
 
 
-def main_kernel(ids_ref, own_ref, twin_ref, rows_ref, own_key_ref, twin_key_ref, code_ref):
+def main_kernel(ids_ref, own_ref, twin_ref, rows_ref, own_key_ref, code_ref, keep_hbm, sem):
+    keep = pltpu.make_async_copy(own_ref, keep_hbm, sem)
+    keep.start()
     core = ids_ref[0]
     mine = ids_ref[1].astype(F32) + 1.0
     tags = tag_rows(own_ref[:, 0:128], CHIPS)
@@ -203,14 +214,13 @@
         return jnp.broadcast_to(jnp.where(label == mine, main_order((MAIN, 1), 0, c), NEVER), (MAIN, 128))
 
     own_key_ref[...] = main_key(tags, core)
-    twin_key_ref[...] = main_key(twin_tags, 1 - core)
+    twin_key = main_key(twin_tags, 1 - core)
     valid = tag_lanes(tags, CHIPS, 0) == mine
     query = jnp.where(valid, main_order((1, MAIN), 1, core), -1.0)
     dest = tag_lanes(tags, CHIPS, 1).astype(I32)
     home = lax.shift_right_logical(dest * 43, 8)
     member = valid & (iota((16, MAIN), 0) == home)
-    before = onehot(iota((MAIN, MAIN), 0) < iota((MAIN, MAIN), 1))
-    ranks = mm(onehot(member), before)
+    ranks = earlier(jnp.where(member, 1.0, 0.0))
     rank = jnp.sum(jnp.where(member, ranks, 0.0), axis=0, keepdims=True)
     rank = jnp.where(valid, rank, -1.0)
     hot = onehot(iota((128, MAIN), 0).astype(F32) == rank)
@@ -222,7 +232,7 @@
     worst = jnp.max(rank, axis=1, keepdims=True)
     found = [
         best(
-            ((own_ref[0:q + 256, :], own_key_ref[0:q + 256, :]), (twin_ref[0:q + 256, :], twin_key_ref[0:q + 256, :])),
+            ((own_ref[0:q + 256, :], own_key_ref[0:q + 256, :]), (twin_ref[0:q + 256, :], twin_key[0:q + 256, :])),
             own_ref[q:q + 256, :],
             query[:, q:q + 256],
         )
@@ -232,32 +242,31 @@
     worst = jnp.broadcast_to(worst, (1, MAIN))
     rows = jnp.concatenate([query, found, home.astype(F32), worst, rank, jnp.zeros((3, MAIN), F32)], axis=0)
     rows_ref[...] = rows
-
-
-def last_kernel(ids_ref, flag_ref, rows_ref, own_key_ref, twin_key_ref, code_ref, own_ref, twin_ref, fix_ref, fix_twin_ref, out_ref):
+    keep.wait()
+
+
+def last_kernel(ids_ref, flag_ref, rows_ref, own_key_ref, code_ref, own_ref, fix_ref, fix_twin_ref, out_ref):
     core = ids_ref[0]
-    fix_tags = tag_rows(fix_ref[:, 0:128], LABELS)
-    fix_twin_tags = tag_rows(fix_twin_ref[:, 0:128], LABELS)
-
-    def fix_key(t, c):
-        valid, chip, at = tag_columns(t, LABELS, (0, 1, 2))
-        return jnp.where(valid > 0.5, fix_order((FIX, 1), 0, c, chip, at), NEVER)
-
     fix_rows = jnp.concatenate([fix_ref[...], fix_twin_ref[...]], axis=0)
-    fix_keys = ((fix_rows, jnp.concatenate([fix_key(fix_tags, core), fix_key(fix_twin_tags, 1 - core)], axis=0)),)
-    fix_valid = tag_lanes(fix_tags, LABELS, 0) > 0.5
-    fix_chip = tag_lanes(fix_tags, LABELS, 1)
-    fix_query = jnp.where(fix_valid, fix_order((1, FIX), 1, core, fix_chip, tag_lanes(fix_tags, LABELS, 2)), -1.0)
-    fix_source = source_of(fix_chip.astype(I32), core).astype(F32)
-    fix_code = jnp.where(fix_valid, fix_source * 128.0 + tag_lanes(fix_tags, LABELS, 3), -1.0)
-    fix_found = best(((own_ref, own_key_ref), (twin_ref, twin_key_ref)) + fix_keys, fix_ref[...], fix_query)
+    orders, queries, codes = [], [], []
+    for ref, c in ((fix_ref, core), (fix_twin_ref, 1 - core)):
+        tags = tag_rows(ref[:, 0:128], LABELS)
+        valid, chip, at = tag_columns(tags, LABELS, (0, 1, 2))
+        orders.append(jnp.where(valid > 0.5, fix_order((FIX, 1), 0, c, chip, at), NEVER))
+        valid = tag_lanes(tags, LABELS, 0) > 0.5
+        chip = tag_lanes(tags, LABELS, 1)
+        queries.append(jnp.where(valid, fix_order((1, FIX), 1, c, chip, tag_lanes(tags, LABELS, 2)), -1.0))
+        source = source_of(chip.astype(I32), c).astype(F32)
+        codes.append(jnp.where(valid, source * 128.0 + tag_lanes(tags, LABELS, 3), -1.0))
+    fix_keys = ((fix_rows, jnp.concatenate(orders, axis=0)),)
+    fix_found = best(((own_ref, own_key_ref),) + fix_keys, fix_rows, jnp.concatenate(queries, axis=1))
     found = jnp.maximum(best(fix_keys, own_ref[...], rows_ref[0:1, :]), rows_ref[1:2, :])
     here = iota((16, MAIN), 0).astype(F32) == rows_ref[2:3, :]
     value = jnp.concatenate([jnp.where(here, part.astype(F32), 0.0).astype(BF) for part in split3(found)], axis=0)
     value = mm_t(value, onehot(iota((128, MAIN), 0).astype(F32) == rows_ref[4:5, :]))
     value = value[0:16] + value[16:32] + value[32:48]
     flag = jnp.maximum(flag_ref[0:1, :], jnp.where(rows_ref[3:4, 0:128] >= 128.0, 1.0, 0.0))
-    common = jnp.concatenate([fix_found, fix_code, flag, jnp.zeros((3, 128), F32)], axis=0)
+    common = jnp.concatenate([lanes_to_rows(fix_found)] + codes + [flag, jnp.zeros((1, 128), F32)], axis=0)
     for m in range(16):
         table = jnp.concatenate([value[m:m + 1], code_ref[m:m + 1], common], axis=0)
         out_ref[m] = table
@@ -310,39 +319,34 @@
 def put_kernel(ids_ref, in_ref, out_ref, flag_ref):
     core = ids_ref[0]
     base = ids_ref[3] * 6
-    val, at = [], []
+    outs = []
     for c in range(2):
+        val, at = [], []
         for k in range(LABELS):
             block = in_ref[c * 16 + core * 8 + k]
-            val.append(block[0:1])
-            at.append(block[1:2].astype(I32))
-            val.append(block[2:3])
-            code = block[3:4].astype(I32)
+            val += [block[0:1], block[2:3], block[3:4]]
+            code = block[4:6].astype(I32)
             q = (code & 127) - base
             ok = (code >= 0) & (q >= 0) & (q < 6)
-            at.append(jnp.where(ok, lax.shift_right_arithmetic(code, 7) * 6 + q, -1))
-    val = jnp.concatenate(val, axis=1)
-    at = jnp.concatenate(at, axis=1)
-    n = val.shape[1]
-    left = jnp.where(iota((8, n), 0) == lax.shift_right_arithmetic(at, 7), val, 0.0)
-    right = onehot(iota((128, n), 0) == (at & 127))
-    out = jnp.zeros((8, 128), F32)
-    for part in split3(left):
-        out = out + mm_t(part, right)
-    out_ref[...] = jnp.maximum(out, -1.0)[0:6]
-    flag = in_ref[0]
-    for i in range(1, 32):
-        flag = jnp.maximum(flag, in_ref[i])
-    flag_ref[...] = flag
-
-
-def call(kernel, shapes, args, flops, memory=pltpu.VMEM, scratch=(), vmem=VMEM, out_memory=pltpu.VMEM):
+            fix_at = jnp.where(ok, lax.shift_right_arithmetic(code, 7) * 6 + q, -1)
+            at += [block[1:2].astype(I32), fix_at[0:1], fix_at[1:2]]
+        val = jnp.concatenate(val, axis=1) + 2.0
+        at = jnp.concatenate(at, axis=1)
+        n = val.shape[1]
+        left = jnp.where(iota((8, n), 0) == lax.shift_right_arithmetic(at, 7), val, 0.0)
+        out = mm_t(jnp.concatenate(split3(left), axis=0), onehot(iota((128, n), 0) == (at & 127)))
+        outs.append(out[0:8] + out[8:16] + out[16:24])
+    out_ref[...] = jnp.maximum(jnp.maximum(outs[0], outs[1]) - 2.0, -1.0)[0:6]
+    flag_ref[0] = jnp.max(jnp.max(in_ref[...], axis=0)[6:7]).astype(I32)
+
+
+def call(kernel, shapes, args, flops, memory=pltpu.VMEM, scratch=(), vmem=VMEM, out_memory=pltpu.VMEM, out_specs=None):
     specs = [pl.BlockSpec(memory_space=pltpu.SMEM)] + [pl.BlockSpec(memory_space=memory)] * (len(args) - 1)
     return pl.pallas_call(
         kernel,
         out_shape=shapes,
         in_specs=specs,
-        out_specs=jax.tree.map(lambda _: pl.BlockSpec(memory_space=out_memory), shapes),
+        out_specs=out_specs or jax.tree.map(lambda _: pl.BlockSpec(memory_space=out_memory), shapes),
         scratch_shapes=scratch,
         compiler_params=pltpu.CompilerParams(vmem_limit_bytes=vmem),
         cost_estimate=pl.CostEstimate(flops=flops, bytes_accessed=4 << 20, transcendentals=0),
@@ -360,7 +364,7 @@
 
 
 def general_path(main, ids, label_of_chip, core):
-    tags = main.reshape(CHIPS, SLOT, D)[:, CAP, :32].astype(F32)
+    tags = main[CAP::SLOT, :32].astype(F32)
     label = tags[:, 0:16].reshape(MAIN)
     dest = tags[:, 16:32].reshape(MAIN)
     slot = jnp.arange(MAIN, dtype=I32)
@@ -387,12 +391,8 @@
     return place(jnp.broadcast_to(table, (32, 24, 128)), ids)
 
 
-def body(embeddings, labels, send_list):
-    core = lax.axis_index("core").astype(I32)
-    member = lax.axis_index(("yh", "yl", "z")).astype(I32)
-    label_of_chip = member & 7
-    ids = jnp.stack([core, label_of_chip, label_of_chip, member])
-    packed = call(
+def pack_call(ids, embeddings, labels, send_list):
+    return call(
         pack_kernel,
         struct((MAIN, D), BF),
         (ids, embeddings, labels, send_list),
@@ -409,28 +409,55 @@
         56 * 1024 * 1024,
         pltpu.HBM,
     )
+
+
+def fix_call(ids, main):
+    return call(fix_kernel, (struct((FIX, D), BF), struct((8, 128), F32)), (ids, main), 1 << 30)
+
+
+def main_call(ids, main, twin):
+    wide = struct((MAIN, 128), F32)
+    shapes = (struct((8, MAIN), F32), wide, struct((16, 128), F32), struct((MAIN, D), BF))
+    specs = tuple(pl.BlockSpec(memory_space=pltpu.VMEM) for _ in range(3)) + (pl.BlockSpec(memory_space=pltpu.HBM),)
+    return call(main_kernel, shapes, (ids, main, twin), 3 << 30, scratch=(pltpu.SemaphoreType.DMA,), out_specs=specs)
+
+
+def last_call(*args):
+    return call(last_kernel, struct((32, 8, 128), F32), args, 1 << 30)
+
+
+def put_call(ids, back):
+    specs = (pl.BlockSpec(memory_space=pltpu.VMEM), pl.BlockSpec(memory_space=pltpu.SMEM))
+    return call(put_kernel, (struct((6, 128), F32), struct((1,), I32)), (ids, back), 1 << 27, out_specs=specs)
+
+
+def body(embeddings, labels, send_list):
+    core = lax.axis_index("core").astype(I32)
+    member = lax.axis_index(("yh", "yl", "z")).astype(I32)
+    label_of_chip = member & 7
+    ids = jnp.stack([core, label_of_chip, label_of_chip, member])
+    packed = pack_call(ids, embeddings, labels, send_list)
     main = lax.all_to_all(
         packed.reshape(CHIPS, SLOT, D), CHIP_AXES, split_axis=0, concat_axis=0, tiled=True
     ).reshape(MAIN, D)
     swap = [(0, 1), (1, 0)]
     twin = lax.ppermute(main, "core", swap)
-    fix, flag = call(fix_kernel, (struct((FIX, D), BF), struct((8, 128), F32)), (ids, main), 1 << 30)
+    fix, flag = fix_call(ids, main)
     fix = lax.all_to_all(
         fix.reshape(LABELS, SLOT, D), GROUP_CHIPS, split_axis=0, concat_axis=0, tiled=True
     ).reshape(FIX, D)
-    wide = struct((MAIN, 128), F32)
-    shapes = (struct((8, MAIN), F32), wide, wide, struct((16, 128), F32))
-    parts = call(main_kernel, shapes, (ids, main, twin), 3 << 30)
-    fix, code = lax.optimization_barrier((fix, parts[3]))
+    parts = main_call(ids, main, twin)
+    fix, code = lax.optimization_barrier((fix, parts[2]))
     fix_twin = lax.ppermute(fix, "core", swap)
-    table = call(last_kernel, struct((32, 8, 128), F32), (ids, flag, *parts[:3], code, main, twin, fix, fix_twin), 1 << 30)
+    table = last_call(ids, flag, *parts[:2], code, main, fix, fix_twin)
     back = lax.all_to_all(table, PLANE, split_axis=0, concat_axis=0, tiled=True)
-    out, flag = call(put_kernel, (struct((6, 128), F32), struct((8, 128), F32)), (ids, back), 1 << 27)
-    return lax.cond(
-        flag[4, 0] > 0.0,
-        lambda: general_path(main, ids, label_of_chip, core),
-        lambda: out.reshape(ROWS),
+    out, flag = put_call(ids, back)
+    _, out = lax.while_loop(
+        lambda state: state[0] > 0,
+        lambda state: (state[0] * 0, general_path(parts[3], ids, label_of_chip, core)),
+        (flag[0], out.reshape(ROWS)),
     )
+    return out
 
 
 def solution(mesh):

time: 84.4 us -> 80.6 us (0.955)
  blocking collectives: 39.8 us -> 51 us
  waiting for transfers between devices: 9.85 us -> 2.28 us
  starting transfers between devices: 11.5 us -> 7.53 us
  Pallas kernels: 20.9 us -> 18.3 us
  local copies, waits for them, and re-layouts: 1.11 us -> 0 us
  loops' own time: 0.01 us -> 0.88 us
    all_to_all x0 -> x1, blocking collectives: none -> 11.3 us  [body(): back = lax.all_to_all(table, PLANE, split_axis=0, concat_axis=0, tiled=True)]
    all_to_all x1 -> x0, waiting for transfers between devices: 7.54 us -> none  [body(): back = lax.all_to_all(table, PLANE, split_axis=0, concat_axis=0, tiled=True)]
    all_to_all x1 -> x0, starting transfers between devices: 3.99 us -> none  [body(): back = lax.all_to_all(table, PLANE, split_axis=0, concat_axis=0, tiled=True)]
    pallas_call x5, Pallas kernels: 20.9 us -> 18.3 us  [call(): pl.pallas_call(kernel, out_shape=shapes, in_specs=specs, out_specs=out_sp...]
    another operation x1, loops' own time: 0.01 us -> 0.88 us  [body(): lax.while_loop(lambda state: state[0] > 0, lambda state: (state[0] * 0, g...]
  transfers between devices with their start and end apart: 4 -> 3, of which waited for: 3 -> 2; matrix products, arithmetic and copies ran while one was open for 0% -> 0% of each run, Pallas kernels for 11% -> 10%
where the time goes in v3:
time: 80.6 us; the launch traced here: 80.2 us
  blocking collectives  51 us (63%)
  Pallas kernels  18.3 us (23%)
  starting transfers between devices  7.53 us (9%)
  waiting for transfers between devices  2.28 us (3%)
  loops' own time  0.88 us (1%)
    all_to_all x1, blocking collectives, body(): lax.all_to_all(packed.reshape(CHIPS, SLOT, D), CHIP_AXES, split_axis=0, c...  39.6 us
    pallas_call x5, Pallas kernels, call(): pl.pallas_call(kernel, out_shape=shapes, in_specs=specs, out_specs=out_sp...  18.3 us
    all_to_all x1, blocking collectives, body(): back = lax.all_to_all(table, PLANE, split_axis=0, concat_axis=0, tiled=True)  11.3 us
    all_to_all x1, starting transfers between devices, body(): lax.all_to_all(fix.reshape(LABELS, SLOT, D), GROUP_CHIPS, split_axis=0, c...  3.41 us
    ppermute x1, starting transfers between devices, body(): twin = lax.ppermute(main, 'core', swap)  2.99 us
  transfers between devices with their start and end apart: 3, of which 2 were waited for; matrix products, arithmetic and copies ran while one was open for 0% of the time, Pallas kernels for 10%

profile of v3, /device:TPU:1, one launch (start us, length us, event | category | flops | bytes accessed | tf_op | source)
XLA Modules:
  0.0 80.2 jit_solution(5869350819243275405)
XLA Ops:
  0.0 0.1 pad_add_fusion.ids_ref
  0.1 6.0 %shard_map.37 = bf16[1024,1024]{1,0:T(8,128)(2,1)} custom-call(s32[4]{0:T(128)S(1)} %pad_add_fusion.ids_ref, bf16[768,1024]{1,0:T(8,128)(2,1)} %emb_hbm.1, s32[768]{0:T(1024)} %lab_hbm.1, s32[1,768]{1,0:T(1,128)} %list_hbm.1), custom_call_target="tpu_custom_call" | custom-call | flops 3221225472 | bytes 4194304 | tf_op jit(solution)/shard_map/pallas_call | solution.py:345
  6.1 39.6 %all_to_all.20 = bf16[64,16,1024]{2,1,0:T(8,128)(2,1)S(1)} all-to-all(bf16[64,16,1024]{2,1,0:T(8,128)(2,1)} %bitcast.37), channel_id=1, replica_groups=mesh['x'=4,'core'=2,'yh'=2,'yl'=2,'z'=4] {'x','yh','yl','z'}, dimensions={0} | all-to-all | bytes 4194304 | tf_op jit(solution)/shard_map/all_to_all | solution.py:440
  45.7 3.0 %collective-permute-start.2 = (bf16[1024,1024]{1,0:T(8,128)(2,1)S(1)}, bf16[1024,1024]{1,0:T(8,128)(2,1)}, u32[]{:S(2)}, u32[]{:S(2)}) collective-permute-start(bf16[1024,1024]{1,0:T(8,128)(2,1)S(1)} %bitcast.27), channel_id=1, source_target_pairs={{0,16},{16,0},{1,17},{17,1},{2,18},{18,2},{3,19},{19,3},{4,20},{20... | collective-permute-start | bytes 6291464 | tf_op jit(solution)/shard_map/ppermute | solution.py:444
  48.7 2.4 %shard_map.38 = (bf16[128,1024]{1,0:T(8,128)(2,1)}, f32[8,128]{1,0:T(8,128)S(1)}) custom-call(s32[4]{0:T(128)S(1)} %pad_add_fusion.ids_ref, bf16[1024,1024]{1,0:T(8,128)(2,1)S(1)} %bitcast.28), custom_call_target="tpu_custom_call" | custom-call | flops 1073741824 | bytes 4194304 | tf_op jit(solution)/shard_map/pallas_call | solution.py:345
  51.0 3.4 %all-to-all-start.2 = ((bf16[8,16,1024]{2,1,0:T(8,128)(2,1)}), bf16[8,16,1024]{2,1,0:T(8,128)(2,1)S(1)}, u32[]{:S(2)}, u32[]{:S(2)}) async-start(bf16[8,16,1024]{2,1,0:T(8,128)(2,1)} %bitcast.6), calls=%async_computation.2 | async-start | bytes 524288 | tf_op jit(solution)/shard_map/all_to_all | solution.py:446
  54.5 0.0 collective-permute-done.2.twin_ref
  54.5 5.6 %shard_map.39 = (f32[8,1024]{1,0:T(8,128)S(1)}, f32[1024,128]{1,0:T(8,128)S(1)}, f32[16,128]{1,0:T(8,128)S(1)}, bf16[1024,1024]{1,0:T(8,128)(2,1)}) custom-call(s32[4]{0:T(128)S(1)} %pad_add_fusion.ids_ref, bf16[1024,1024]{1,0:T(8,128)(2,1)S(1)} %bitcast.29, bf16[1024,1024]{1,0:T(8,128)(2,1)} %collective-permute-done.2.twin_ref), custom_call_target="tpu_custom_call" | custom-call | flops 3221225472 | bytes 4194304 | tf_op jit(solution)/shard_map/pallas_call | solution.py:345
  60.1 1.1 %all-to-all-done.2 = bf16[8,16,1024]{2,1,0:T(8,128)(2,1)S(1)} async-done(((bf16[8,16,1024]{2,1,0:T(8,128)(2,1)}), bf16[8,16,1024]{2,1,0:T(8,128)(2,1)S(1)}, u32[]{:S(2)}, u32[]{:S(2)}) %all-to-all-start.2) | async-done | bytes 262176 | tf_op jit(solution)/shard_map/all_to_all | solution.py:446
  61.2 1.1 %collective-permute-start.3 = (bf16[128,1024]{1,0:T(8,128)(2,1)S(1)}, bf16[128,1024]{1,0:T(8,128)(2,1)S(1)}, u32[]{:S(2)}, u32[]{:S(2)}) collective-permute-start(bf16[128,1024]{1,0:T(8,128)(2,1)S(1)} %bitcast.31), channel_id=1, source_target_pairs={{0,16},{16,0},{1,17},{17,1},{2,18},{18,2},{3,19},{19,3},{4,20},{20... | collective-permute-start | bytes 786440 | tf_op jit(solution)/shard_map/ppermute | solution.py:451
  62.3 1.2 %collective-permute-done.3.fix_twin_ref = bf16[128,1024]{1,0:T(8,128)(2,1)S(1)} collective-permute-done((bf16[128,1024]{1,0:T(8,128)(2,1)S(1)}, bf16[128,1024]{1,0:T(8,128)(2,1)S(1)}, u32[]{:S(2)}, u32[]{:S(2)}) %collective-permute-start.3) | collective-permute-done | bytes 262176 | tf_op jit(solution)/shard_map/ppermute | solution.py:451
  63.5 2.5 %shard_map.40 = f32[32,8,128]{2,1,0:T(8,128)S(1)} custom-call(s32[4]{0:T(128)S(1)} %pad_add_fusion.ids_ref, f32[8,128]{1,0:T(8,128)S(1)} %get-tuple-element.101.flag_ref, f32[8,1024]{1,0:T(8,128)S(1)} %get-tuple-element.102.rows_ref, f32[1024,128]{1,0:T(8,128)S(1)} %get-tuple-element.103.own_key_ref, f32[16,128]{1,0:T(8,128)S(1)} %get-tuple-element.106.code_ref, ...), custom_call_target="tpu_custom_call" | custom-call | flops 1073741824 | bytes 4194304 | tf_op jit(solution)/shard_map/pallas_call | solution.py:345
  66.0 11.3 %all_to_all.21.in_ref = f32[32,8,128]{2,1,0:T(8,128)S(1)} all-to-all(f32[32,8,128]{2,1,0:T(8,128)S(1)} %shard_map.40), channel_id=1, replica_groups=mesh['x'=4,'core'=2,'yh'=2,'yl'=2,'z'=4] {'core','yh','yl','z'}, dimensions={0} | all-to-all | bytes 262144 | tf_op jit(solution)/shard_map/all_to_all | solution.py:453
  77.3 1.8 %shard_map.41 = (f32[6,128]{1,0:T(8,128)}, s32[1]{0:T(128)}) custom-call(s32[4]{0:T(128)S(1)} %pad_add_fusion.ids_ref, f32[32,8,128]{2,1,0:T(8,128)S(1)} %all_to_all.21.in_ref), custom_call_target="tpu_custom_call" | custom-call | flops 134217728 | bytes 4194304 | tf_op jit(solution)/shard_map/pallas_call | solution.py:345
  79.1 0.9 %while.24 = (s32[]{:T(128)}, f32[768]{0:T(1024)}, bf16[1024,1024]{1,0:T(8,128)(2,1)}, s32[]{:T(128)}, s32[]{:T(128)}, /*index=5*/s32[4]{0:T(128)S(1)}) while((s32[]{:T(128)}, f32[768]{0:T(1024)}, bf16[1024,1024]{1,0:T(8,128)(2,1)}, s32[]{:T(128)}, s32[]{:T(128)}, /*index=5*/s32[4]{0:T(128)S(1)}) %tuple.49), condition=%region_4.5_spmd, body=%region_0.4_spmd | while | flops 2287025152 | bytes 26602164 | solution.py:455
Async XLA Ops:
  45.7 8.8 %collective-permute-start.2 = (bf16[1024,1024]{1,0:T(8,128)(2,1)S(1)}, bf16[1024,1024]{1,0:T(8,128)(2,1)}, u32[]{:S(2)}, u32[]{:S(2)}) collective-permute-start(bf16[1024,1024]{1,0:T(8,128)(2,1)S(1)} %bitcast.27), channel_id=1, source_target_pairs={{0,16},{16,0},{1,17},{17,1},{2,18},{18,2},{3,19},{19,3},{4,20},{20... | collective-permute-start | bytes 6291464 | tf_op jit(solution)/shard_map/ppermute | solution.py:444
  51.0 10.1 %all-to-all-start.2 = ((bf16[8,16,1024]{2,1,0:T(8,128)(2,1)}), bf16[8,16,1024]{2,1,0:T(8,128)(2,1)S(1)}, u32[]{:S(2)}, u32[]{:S(2)}) async-start(bf16[8,16,1024]{2,1,0:T(8,128)(2,1)} %bitcast.6), calls=%async_computation.2 | async-start | bytes 524288 | tf_op jit(solution)/shard_map/all_to_all | solution.py:446
  61.2 2.3 %collective-permute-start.3 = (bf16[128,1024]{1,0:T(8,128)(2,1)S(1)}, bf16[128,1024]{1,0:T(8,128)(2,1)S(1)}, u32[]{:S(2)}, u32[]{:S(2)}) collective-permute-start(bf16[128,1024]{1,0:T(8,128)(2,1)S(1)} %bitcast.31), channel_id=1, source_target_pairs={{0,16},{16,0},{1,17},{17,1},{2,18},{18,2},{3,19},{19,3},{4,20},{20... | collective-permute-start | bytes 786440 | tf_op jit(solution)/shard_map/ppermute | solution.py:451

commit v4 on v3

--- a/solution.py
+++ b/solution.py
@@ -55,7 +55,7 @@
     return jnp.concatenate([inside[i * n:(i + 1) * n] for i in range(parts)], axis=1)
 
 
-def pack_kernel(ids_ref, emb_hbm, lab_hbm, list_hbm, out_hbm, emb_ref, lab_ref, list_ref, out_ref, sems, out_sems):
+def pack_kernel(ids_ref, emb_hbm, lab_hbm, list_hbm, out_ref, emb_ref, lab_ref, list_ref, sems):
     copies = [
         pltpu.make_async_copy(src, dst, sems.at[i])
         for i, (src, dst) in enumerate(((list_hbm, list_ref), (lab_hbm, lab_ref), (emb_hbm, emb_ref)))
@@ -107,18 +107,10 @@
     tags = jnp.where(lane < 16, label + 1.0, jnp.where(lane < 32, dest, 0.0)).astype(BF)
     tag = jnp.where((iota((MAIN, 128), 1) & 15) == (slot & 15), mm_t(pick, tags), 0.0)
     tag = jnp.broadcast_to(jnp.sum(tag.reshape(CHIPS, SLOT, 128), axis=1, keepdims=True), (CHIPS, SLOT, 128)).reshape(MAIN, 128)
-    copies = []
-    for i, b in enumerate(range(0, D, 256)):
-        part = mm(pick, unit[:, b:b + 256])
-        if b == 0:
-            out_ref[:, 0:128] = jnp.where(at >= CAP, tag, part[:, 0:128]).astype(BF)
-            out_ref[:, 128:256] = part[:, 128:256].astype(BF)
-        else:
-            out_ref[:, b:b + 256] = part.astype(BF)
-        copies.append(pltpu.make_async_copy(out_ref.at[:, b:b + 256], out_hbm.at[:, b:b + 256], out_sems.at[i]))
-        copies[-1].start()
-    for copy in copies:
-        copy.wait()
+    for r in range(0, MAIN, 256):
+        part = mm(pick[r:r + 256], unit)
+        out_ref[r:r + 256, 0:128] = jnp.where(at[r:r + 256] >= CAP, tag[r:r + 256], part[:, 0:128]).astype(BF)
+        out_ref[r:r + 256, 128:D] = part[:, 128:D].astype(BF)
 
 
 def tag_rows(first, n):
@@ -160,11 +152,13 @@
     return away_order(source_of(chip, core), (holder - chip) & 7, at.astype(I32))
 
 
-def fix_kernel(ids_ref, main_ref, out_ref, flag_ref):
+def fix_kernel(ids_ref, main_ref, out_ref, flag_ref, tags_ref, lanes_ref):
     own = ids_ref[1].astype(F32)
     tags = tag_rows(main_ref[:, 0:128], CHIPS)
     label = tag_lanes(tags, CHIPS, 0)
     dest = tag_lanes(tags, CHIPS, 1)
+    tags_ref[...] = tags
+    lanes_ref[...] = jnp.concatenate([label, dest, jnp.zeros((6, MAIN), F32)], axis=0)
     moved = (label > 0.5) & (label != own + 1.0)
     member = moved & (iota((LABELS, MAIN), 0).astype(F32) == label - 1.0)
     ranks = earlier(jnp.where(member, 1.0, 0.0))
@@ -201,23 +195,20 @@
     return found
 
 
-def main_kernel(ids_ref, own_ref, twin_ref, rows_ref, own_key_ref, code_ref, keep_hbm, sem):
-    keep = pltpu.make_async_copy(own_ref, keep_hbm, sem)
-    keep.start()
+def main_kernel(ids_ref, tags_ref, lanes_ref, own_ref, twin_ref, rows_ref, own_key_ref, code_ref):
     core = ids_ref[0]
     mine = ids_ref[1].astype(F32) + 1.0
-    tags = tag_rows(own_ref[:, 0:128], CHIPS)
     twin_tags = tag_rows(twin_ref[:, 0:128], CHIPS)
 
     def main_key(t, c):
         (label,) = tag_columns(t, CHIPS, (0,))
         return jnp.broadcast_to(jnp.where(label == mine, main_order((MAIN, 1), 0, c), NEVER), (MAIN, 128))
 
-    own_key_ref[...] = main_key(tags, core)
+    own_key_ref[...] = main_key(tags_ref[...], core)
     twin_key = main_key(twin_tags, 1 - core)
-    valid = tag_lanes(tags, CHIPS, 0) == mine
+    valid = lanes_ref[0:1, :] == mine
     query = jnp.where(valid, main_order((1, MAIN), 1, core), -1.0)
-    dest = tag_lanes(tags, CHIPS, 1).astype(I32)
+    dest = lanes_ref[1:2, :].astype(I32)
     home = lax.shift_right_logical(dest * 43, 8)
     member = valid & (iota((16, MAIN), 0) == home)
     ranks = earlier(jnp.where(member, 1.0, 0.0))
@@ -242,7 +233,6 @@
     worst = jnp.broadcast_to(worst, (1, MAIN))
     rows = jnp.concatenate([query, found, home.astype(F32), worst, rank, jnp.zeros((3, MAIN), F32)], axis=0)
     rows_ref[...] = rows
-    keep.wait()
 
 
 def last_kernel(ids_ref, flag_ref, rows_ref, own_key_ref, code_ref, own_ref, fix_ref, fix_twin_ref, out_ref):
@@ -391,35 +381,32 @@
     return place(jnp.broadcast_to(table, (32, 24, 128)), ids)
 
 
-def pack_call(ids, embeddings, labels, send_list):
+def pack_call(ids, *arrays):
+    arrays = [pltpu.with_memory_space_constraint(array, pltpu.HBM) for array in arrays]
     return call(
         pack_kernel,
         struct((MAIN, D), BF),
-        (ids, embeddings, labels, send_list),
+        (ids, *arrays),
         3 << 30,
-        pltpu.HBM,
+        pl.ANY,
         (
             pltpu.VMEM((ROWS, D), BF),
             pltpu.VMEM((ROWS,), I32),
             pltpu.VMEM((1, ROWS), I32),
-            pltpu.VMEM((MAIN, D), BF),
             pltpu.SemaphoreType.DMA((3,)),
-            pltpu.SemaphoreType.DMA((4,)),
         ),
-        56 * 1024 * 1024,
-        pltpu.HBM,
     )
 
 
 def fix_call(ids, main):
-    return call(fix_kernel, (struct((FIX, D), BF), struct((8, 128), F32)), (ids, main), 1 << 30)
-
-
-def main_call(ids, main, twin):
+    shapes = (struct((FIX, D), BF), struct((8, 128), F32), struct((CHIPS, 128), BF), struct((8, MAIN), F32))
+    return call(fix_kernel, shapes, (ids, main), 1 << 30)
+
+
+def main_call(*args):
     wide = struct((MAIN, 128), F32)
-    shapes = (struct((8, MAIN), F32), wide, struct((16, 128), F32), struct((MAIN, D), BF))
-    specs = tuple(pl.BlockSpec(memory_space=pltpu.VMEM) for _ in range(3)) + (pl.BlockSpec(memory_space=pltpu.HBM),)
-    return call(main_kernel, shapes, (ids, main, twin), 3 << 30, scratch=(pltpu.SemaphoreType.DMA,), out_specs=specs)
+    shapes = (struct((8, MAIN), F32), wide, struct((16, 128), F32))
+    return call(main_kernel, shapes, args, 3 << 30)
 
 
 def last_call(*args):
@@ -442,11 +429,11 @@
     ).reshape(MAIN, D)
     swap = [(0, 1), (1, 0)]
     twin = lax.ppermute(main, "core", swap)
-    fix, flag = fix_call(ids, main)
+    fix, flag, tags, lanes = fix_call(ids, main)
     fix = lax.all_to_all(
         fix.reshape(LABELS, SLOT, D), GROUP_CHIPS, split_axis=0, concat_axis=0, tiled=True
     ).reshape(FIX, D)
-    parts = main_call(ids, main, twin)
+    parts = main_call(ids, tags, lanes, main, twin)
     fix, code = lax.optimization_barrier((fix, parts[2]))
     fix_twin = lax.ppermute(fix, "core", swap)
     table = last_call(ids, flag, *parts[:2], code, main, fix, fix_twin)
@@ -454,7 +441,7 @@
     out, flag = put_call(ids, back)
     _, out = lax.while_loop(
         lambda state: state[0] > 0,
-        lambda state: (state[0] * 0, general_path(parts[3], ids, label_of_chip, core)),
+        lambda state: (state[0] * 0, general_path(lax.ppermute(twin, "core", swap), ids, label_of_chip, core)),
         (flag[0], out.reshape(ROWS)),
     )
     return out

time: 80.6 us -> 78.8 us (0.978)
  Pallas kernels: 18.3 us -> 16.8 us
    pallas_call x5, Pallas kernels: 18.3 us -> 16.8 us  [call(): pl.pallas_call(kernel, out_shape=shapes, in_specs=specs, out_specs=out_sp...]
where the time goes in v4:
time: 78.8 us; the launch traced here: 78.5 us
  blocking collectives  50.4 us (64%)
  Pallas kernels  16.8 us (21%)
  starting transfers between devices  7.47 us (9%)
  waiting for transfers between devices  2.72 us (3%)
  loops' own time  0.81 us (1%)
    all_to_all x1, blocking collectives, body(): lax.all_to_all(packed.reshape(CHIPS, SLOT, D), CHIP_AXES, split_axis=0, c...  39.5 us
    pallas_call x5, Pallas kernels, call(): pl.pallas_call(kernel, out_shape=shapes, in_specs=specs, out_specs=out_sp...  16.8 us
    all_to_all x1, blocking collectives, body(): back = lax.all_to_all(table, PLANE, split_axis=0, concat_axis=0, tiled=True)  10.9 us
    all_to_all x1, starting transfers between devices, body(): lax.all_to_all(fix.reshape(LABELS, SLOT, D), GROUP_CHIPS, split_axis=0, c...  3.41 us
    ppermute x1, starting transfers between devices, body(): twin = lax.ppermute(main, 'core', swap)  2.94 us
  transfers between devices with their start and end apart: 3, of which 2 were waited for; matrix products, arithmetic and copies ran while one was open for 0% of the time, Pallas kernels for 10%

profile of v4, /device:TPU:1, one launch (start us, length us, event | category | flops | bytes accessed | tf_op | source)
XLA Modules:
  0.0 78.5 jit_solution(1017830831318078531)
XLA Ops:
  0.0 0.1 pad_add_fusion.ids_ref
  0.1 5.0 %shard_map.37 = bf16[1024,1024]{1,0:T(8,128)(2,1)S(1)} custom-call(s32[4]{0:T(128)S(1)} %pad_add_fusion.ids_ref, bf16[768,1024]{1,0:T(8,128)(2,1)} %emb_hbm.1, s32[768]{0:T(1024)} %lab_hbm.1, s32[1,768]{1,0:T(1,128)} %list_hbm.1), custom_call_target="tpu_custom_call" | custom-call | flops 3221225472 | bytes 4194304 | tf_op jit(solution)/shard_map/pallas_call | solution.py:335
  5.1 39.5 %all_to_all.20 = bf16[64,16,1024]{2,1,0:T(8,128)(2,1)S(1)} all-to-all(bf16[64,16,1024]{2,1,0:T(8,128)(2,1)S(1)} %bitcast.31), channel_id=1, replica_groups=mesh['x'=4,'core'=2,'yh'=2,'yl'=2,'z'=4] {'x','yh','yl','z'}, dimensions={0} | all-to-all | bytes 4194304 | tf_op jit(solution)/shard_map/all_to_all | solution.py:427
  44.6 2.9 %collective-permute-start.3 = (bf16[1024,1024]{1,0:T(8,128)(2,1)S(1)}, bf16[1024,1024]{1,0:T(8,128)(2,1)}, u32[]{:S(2)}, u32[]{:S(2)}) collective-permute-start(bf16[1024,1024]{1,0:T(8,128)(2,1)S(1)} %bitcast.27), channel_id=1, source_target_pairs={{0,16},{16,0},{1,17},{17,1},{2,18},{18,2},{3,19},{19,3},{4,20},{20... | collective-permute-start | bytes 6291464 | tf_op jit(solution)/shard_map/ppermute | solution.py:431
  47.5 2.3 %shard_map.38 = (bf16[128,1024]{1,0:T(8,128)(2,1)}, f32[8,128]{1,0:T(8,128)S(1)}, bf16[64,128]{1,0:T(8,128)(2,1)S(1)}, f32[8,1024]{1,0:T(8,128)S(1)}) custom-call(s32[4]{0:T(128)S(1)} %pad_add_fusion.ids_ref, bf16[1024,1024]{1,0:T(8,128)(2,1)S(1)} %bitcast.28), custom_call_target="tpu_custom_call" | custom-call | flops 1073741824 | bytes 4194304 | tf_op jit(solution)/shard_map/pallas_call | solution.py:335
  49.9 3.4 %all-to-all-start.2 = ((bf16[8,16,1024]{2,1,0:T(8,128)(2,1)}), bf16[8,16,1024]{2,1,0:T(8,128)(2,1)S(1)}, u32[]{:S(2)}, u32[]{:S(2)}) async-start(bf16[8,16,1024]{2,1,0:T(8,128)(2,1)} %bitcast.6), calls=%async_computation.2 | async-start | bytes 524288 | tf_op jit(solution)/shard_map/all_to_all | solution.py:433
  53.3 0.0 collective-permute-done.3.twin_ref
  53.3 5.2 %shard_map.39 = (f32[8,1024]{1,0:T(8,128)S(1)}, f32[1024,128]{1,0:T(8,128)S(1)}, f32[16,128]{1,0:T(8,128)S(1)}) custom-call(s32[4]{0:T(128)S(1)} %pad_add_fusion.ids_ref, bf16[64,128]{1,0:T(8,128)(2,1)S(1)} %get-tuple-element.103.tags_ref, f32[8,1024]{1,0:T(8,128)S(1)} %get-tuple-element.104.lanes_ref, bf16[1024,1024]{1,0:T(8,128)(2,1)S(1)} %bitcast.29, ...), custom_call_target="tpu_custom_call" | custom-call | flops 3221225472 | bytes 4194304 | tf_op jit(solution)/shard_map/pallas_call | solution.py:335
  58.5 1.6 %all-to-all-done.2 = bf16[8,16,1024]{2,1,0:T(8,128)(2,1)S(1)} async-done(((bf16[8,16,1024]{2,1,0:T(8,128)(2,1)}), bf16[8,16,1024]{2,1,0:T(8,128)(2,1)S(1)}, u32[]{:S(2)}, u32[]{:S(2)}) %all-to-all-start.2) | async-done | bytes 262176 | tf_op jit(solution)/shard_map/all_to_all | solution.py:433
  60.0 1.1 %collective-permute-start.4 = (bf16[128,1024]{1,0:T(8,128)(2,1)S(1)}, bf16[128,1024]{1,0:T(8,128)(2,1)S(1)}, u32[]{:S(2)}, u32[]{:S(2)}) collective-permute-start(bf16[128,1024]{1,0:T(8,128)(2,1)S(1)} %bitcast.32), channel_id=1, source_target_pairs={{0,16},{16,0},{1,17},{17,1},{2,18},{18,2},{3,19},{19,3},{4,20},{20... | collective-permute-start | bytes 786440 | tf_op jit(solution)/shard_map/ppermute | solution.py:438
  61.1 1.2 %collective-permute-done.4.fix_twin_ref = bf16[128,1024]{1,0:T(8,128)(2,1)S(1)} collective-permute-done((bf16[128,1024]{1,0:T(8,128)(2,1)S(1)}, bf16[128,1024]{1,0:T(8,128)(2,1)S(1)}, u32[]{:S(2)}, u32[]{:S(2)}) %collective-permute-start.4) | collective-permute-done | bytes 262176 | tf_op jit(solution)/shard_map/ppermute | solution.py:438
  62.3 2.5 %shard_map.40 = f32[32,8,128]{2,1,0:T(8,128)S(1)} custom-call(s32[4]{0:T(128)S(1)} %pad_add_fusion.ids_ref, f32[8,128]{1,0:T(8,128)S(1)} %get-tuple-element.102.flag_ref, f32[8,1024]{1,0:T(8,128)S(1)} %get-tuple-element.105.rows_ref, f32[1024,128]{1,0:T(8,128)S(1)} %get-tuple-element.106.own_key_ref, f32[16,128]{1,0:T(8,128)S(1)} %get-tuple-element.109.code_ref, ...), custom_call_target="tpu_custom_call" | custom-call | flops 1073741824 | bytes 4194304 | tf_op jit(solution)/shard_map/pallas_call | solution.py:335
  64.8 10.9 %all_to_all.21.in_ref = f32[32,8,128]{2,1,0:T(8,128)S(1)} all-to-all(f32[32,8,128]{2,1,0:T(8,128)S(1)} %shard_map.40), channel_id=1, replica_groups=mesh['x'=4,'core'=2,'yh'=2,'yl'=2,'z'=4] {'core','yh','yl','z'}, dimensions={0} | all-to-all | bytes 262144 | tf_op jit(solution)/shard_map/all_to_all | solution.py:440
  75.7 1.8 %shard_map.41 = (f32[6,128]{1,0:T(8,128)}, s32[1]{0:T(128)}) custom-call(s32[4]{0:T(128)S(1)} %pad_add_fusion.ids_ref, f32[32,8,128]{2,1,0:T(8,128)S(1)} %all_to_all.21.in_ref), custom_call_target="tpu_custom_call" | custom-call | flops 134217728 | bytes 4194304 | tf_op jit(solution)/shard_map/pallas_call | solution.py:335
  77.5 0.8 %while.24 = (s32[]{:T(128)}, f32[768]{0:T(1024)}, bf16[1024,1024]{1,0:T(8,128)(2,1)}, s32[]{:T(128)}, s32[]{:T(128)}, /*index=5*/s32[4]{0:T(128)S(1)}) while((s32[]{:T(128)}, f32[768]{0:T(1024)}, bf16[1024,1024]{1,0:T(8,128)(2,1)}, s32[]{:T(128)}, s32[]{:T(128)}, /*index=5*/s32[4]{0:T(128)S(1)}) %tuple.50), condition=%region_4.5_spmd, body=%region_0.4_spmd | while | flops 2287025152 | bytes 43379448 | solution.py:442
Async XLA Ops:
  44.6 8.7 %collective-permute-start.3 = (bf16[1024,1024]{1,0:T(8,128)(2,1)S(1)}, bf16[1024,1024]{1,0:T(8,128)(2,1)}, u32[]{:S(2)}, u32[]{:S(2)}) collective-permute-start(bf16[1024,1024]{1,0:T(8,128)(2,1)S(1)} %bitcast.27), channel_id=1, source_target_pairs={{0,16},{16,0},{1,17},{17,1},{2,18},{18,2},{3,19},{19,3},{4,20},{20... | collective-permute-start | bytes 6291464 | tf_op jit(solution)/shard_map/ppermute | solution.py:431
  49.9 10.2 %all-to-all-start.2 = ((bf16[8,16,1024]{2,1,0:T(8,128)(2,1)}), bf16[8,16,1024]{2,1,0:T(8,128)(2,1)S(1)}, u32[]{:S(2)}, u32[]{:S(2)}) async-start(bf16[8,16,1024]{2,1,0:T(8,128)(2,1)} %bitcast.6), calls=%async_computation.2 | async-start | bytes 524288 | tf_op jit(solution)/shard_map/all_to_all | solution.py:433
  60.0 2.3 %collective-permute-start.4 = (bf16[128,1024]{1,0:T(8,128)(2,1)S(1)}, bf16[128,1024]{1,0:T(8,128)(2,1)S(1)}, u32[]{:S(2)}, u32[]{:S(2)}) collective-permute-start(bf16[128,1024]{1,0:T(8,128)(2,1)S(1)} %bitcast.32), channel_id=1, source_target_pairs={{0,16},{16,0},{1,17},{17,1},{2,18},{18,2},{3,19},{19,3},{4,20},{20... | collective-permute-start | bytes 786440 | tf_op jit(solution)/shard_map/ppermute | solution.py:438

commit v5 on v4

--- a/solution.py
+++ b/solution.py
@@ -238,29 +238,33 @@
 def last_kernel(ids_ref, flag_ref, rows_ref, own_key_ref, code_ref, own_ref, fix_ref, fix_twin_ref, out_ref):
     core = ids_ref[0]
     fix_rows = jnp.concatenate([fix_ref[...], fix_twin_ref[...]], axis=0)
-    orders, queries, codes = [], [], []
-    for ref, c in ((fix_ref, core), (fix_twin_ref, 1 - core)):
-        tags = tag_rows(ref[:, 0:128], LABELS)
-        valid, chip, at = tag_columns(tags, LABELS, (0, 1, 2))
-        orders.append(jnp.where(valid > 0.5, fix_order((FIX, 1), 0, c, chip, at), NEVER))
-        valid = tag_lanes(tags, LABELS, 0) > 0.5
-        chip = tag_lanes(tags, LABELS, 1)
-        queries.append(jnp.where(valid, fix_order((1, FIX), 1, c, chip, tag_lanes(tags, LABELS, 2)), -1.0))
-        source = source_of(chip.astype(I32), c).astype(F32)
-        codes.append(jnp.where(valid, source * 128.0 + tag_lanes(tags, LABELS, 3), -1.0))
-    fix_keys = ((fix_rows, jnp.concatenate(orders, axis=0)),)
-    fix_found = best(((own_ref, own_key_ref),) + fix_keys, fix_rows, jnp.concatenate(queries, axis=1))
+    tags = tag_rows(fix_rows[:, 0:128], 2 * LABELS)
+
+    def side(shape, dim):
+        return core ^ lax.shift_right_logical(iota(shape, dim), 7)
+
+    tall, wide = (2 * FIX, 1), (1, 2 * FIX)
+    valid, chip, at = tag_columns(tags, 2 * LABELS, (0, 1, 2))
+    fix_keys = ((fix_rows, jnp.where(valid > 0.5, fix_order(tall, 0, side(tall, 0), chip, at), NEVER)),)
+    valid, chip, at, dest = (tag_lanes(tags, 2 * LABELS, k) for k in range(4))
+    source = source_of(chip.astype(I32), side(wide, 1)).astype(F32)
+    fix_query = jnp.where(valid > 0.5, fix_order(wide, 1, side(wide, 1), chip, at), -1.0)
+    fix_code = jnp.where(valid > 0.5, source * 128.0 + dest, -1.0)
+    fix_found = best(((own_ref, own_key_ref),) + fix_keys, fix_rows, fix_query)
     found = jnp.maximum(best(fix_keys, own_ref[...], rows_ref[0:1, :]), rows_ref[1:2, :])
     here = iota((16, MAIN), 0).astype(F32) == rows_ref[2:3, :]
     value = jnp.concatenate([jnp.where(here, part.astype(F32), 0.0).astype(BF) for part in split3(found)], axis=0)
     value = mm_t(value, onehot(iota((128, MAIN), 0).astype(F32) == rows_ref[4:5, :]))
     value = value[0:16] + value[16:32] + value[32:48]
     flag = jnp.maximum(flag_ref[0:1, :], jnp.where(rows_ref[3:4, 0:128] >= 128.0, 1.0, 0.0))
-    common = jnp.concatenate([lanes_to_rows(fix_found)] + codes + [flag, jnp.zeros((1, 128), F32)], axis=0)
-    for m in range(16):
-        table = jnp.concatenate([value[m:m + 1], code_ref[m:m + 1], common], axis=0)
-        out_ref[m] = table
-        out_ref[16 + m] = table
+    common = [lanes_to_rows(fix_found), lanes_to_rows(fix_code), flag, jnp.zeros((1, 128), F32)]
+    common = jnp.concatenate(common, axis=0)
+    shape = (16, 8, 128)
+    row = iota(shape, 1)
+    table = jnp.broadcast_to(jnp.concatenate([jnp.zeros((2, 128), F32), common], axis=0)[None], shape)
+    table = jnp.where(row == 0, value[:, None, :], jnp.where(row == 1, code_ref[...][:, None, :], table))
+    out_ref[0:16] = table
+    out_ref[16:32] = table
 
 
 def split3(v):

time: 78.8 us -> 78.7 us (level)
  no operation moved by 1% of the time
where the time goes in v5:
time: 78.7 us; the launch traced here: 78.3 us
  blocking collectives  50.4 us (64%)
  Pallas kernels  16.7 us (21%)
  starting transfers between devices  7.47 us (9%)
  waiting for transfers between devices  2.72 us (3%)
  loops' own time  0.81 us (1%)
    all_to_all x1, blocking collectives, body(): lax.all_to_all(packed.reshape(CHIPS, SLOT, D), CHIP_AXES, split_axis=0, c...  39.5 us
    pallas_call x5, Pallas kernels, call(): pl.pallas_call(kernel, out_shape=shapes, in_specs=specs, out_specs=out_sp...  16.7 us
    all_to_all x1, blocking collectives, body(): back = lax.all_to_all(table, PLANE, split_axis=0, concat_axis=0, tiled=True)  10.9 us
    all_to_all x1, starting transfers between devices, body(): lax.all_to_all(fix.reshape(LABELS, SLOT, D), GROUP_CHIPS, split_axis=0, c...  3.41 us
    ppermute x1, starting transfers between devices, body(): twin = lax.ppermute(main, 'core', swap)  2.94 us
  transfers between devices with their start and end apart: 3, of which 2 were waited for; matrix products, arithmetic and copies ran while one was open for 0% of the time, Pallas kernels for 10%

profile of v5, /device:TPU:1, one launch (start us, length us, event | category | flops | bytes accessed | tf_op | source)
XLA Modules:
  0.0 78.3 jit_solution(5757489836647870721)
XLA Ops:
  0.0 0.1 pad_add_fusion.ids_ref
  0.1 5.0 %shard_map.37 = bf16[1024,1024]{1,0:T(8,128)(2,1)S(1)} custom-call(s32[4]{0:T(128)S(1)} %pad_add_fusion.ids_ref, bf16[768,1024]{1,0:T(8,128)(2,1)} %emb_hbm.1, s32[768]{0:T(1024)} %lab_hbm.1, s32[1,768]{1,0:T(1,128)} %list_hbm.1), custom_call_target="tpu_custom_call" | custom-call | flops 3221225472 | bytes 4194304 | tf_op jit(solution)/shard_map/pallas_call | solution.py:339
  5.1 39.5 %all_to_all.20 = bf16[64,16,1024]{2,1,0:T(8,128)(2,1)S(1)} all-to-all(bf16[64,16,1024]{2,1,0:T(8,128)(2,1)S(1)} %bitcast.31), channel_id=1, replica_groups=mesh['x'=4,'core'=2,'yh'=2,'yl'=2,'z'=4] {'x','yh','yl','z'}, dimensions={0} | all-to-all | bytes 4194304 | tf_op jit(solution)/shard_map/all_to_all | solution.py:431
  44.6 2.9 %collective-permute-start.3 = (bf16[1024,1024]{1,0:T(8,128)(2,1)S(1)}, bf16[1024,1024]{1,0:T(8,128)(2,1)}, u32[]{:S(2)}, u32[]{:S(2)}) collective-permute-start(bf16[1024,1024]{1,0:T(8,128)(2,1)S(1)} %bitcast.27), channel_id=1, source_target_pairs={{0,16},{16,0},{1,17},{17,1},{2,18},{18,2},{3,19},{19,3},{4,20},{20... | collective-permute-start | bytes 6291464 | tf_op jit(solution)/shard_map/ppermute | solution.py:435
  47.5 2.3 %shard_map.38 = (bf16[128,1024]{1,0:T(8,128)(2,1)}, f32[8,128]{1,0:T(8,128)S(1)}, bf16[64,128]{1,0:T(8,128)(2,1)S(1)}, f32[8,1024]{1,0:T(8,128)S(1)}) custom-call(s32[4]{0:T(128)S(1)} %pad_add_fusion.ids_ref, bf16[1024,1024]{1,0:T(8,128)(2,1)S(1)} %bitcast.28), custom_call_target="tpu_custom_call" | custom-call | flops 1073741824 | bytes 4194304 | tf_op jit(solution)/shard_map/pallas_call | solution.py:339
  49.9 3.4 %all-to-all-start.2 = ((bf16[8,16,1024]{2,1,0:T(8,128)(2,1)}), bf16[8,16,1024]{2,1,0:T(8,128)(2,1)S(1)}, u32[]{:S(2)}, u32[]{:S(2)}) async-start(bf16[8,16,1024]{2,1,0:T(8,128)(2,1)} %bitcast.6), calls=%async_computation.2 | async-start | bytes 524288 | tf_op jit(solution)/shard_map/all_to_all | solution.py:437
  53.3 0.0 collective-permute-done.3.twin_ref
  53.3 5.2 %shard_map.39 = (f32[8,1024]{1,0:T(8,128)S(1)}, f32[1024,128]{1,0:T(8,128)S(1)}, f32[16,128]{1,0:T(8,128)S(1)}) custom-call(s32[4]{0:T(128)S(1)} %pad_add_fusion.ids_ref, bf16[64,128]{1,0:T(8,128)(2,1)S(1)} %get-tuple-element.103.tags_ref, f32[8,1024]{1,0:T(8,128)S(1)} %get-tuple-element.104.lanes_ref, bf16[1024,1024]{1,0:T(8,128)(2,1)S(1)} %bitcast.29, ...), custom_call_target="tpu_custom_call" | custom-call | flops 3221225472 | bytes 4194304 | tf_op jit(solution)/shard_map/pallas_call | solution.py:339
  58.5 1.6 %all-to-all-done.2 = bf16[8,16,1024]{2,1,0:T(8,128)(2,1)S(1)} async-done(((bf16[8,16,1024]{2,1,0:T(8,128)(2,1)}), bf16[8,16,1024]{2,1,0:T(8,128)(2,1)S(1)}, u32[]{:S(2)}, u32[]{:S(2)}) %all-to-all-start.2) | async-done | bytes 262176 | tf_op jit(solution)/shard_map/all_to_all | solution.py:437
  60.0 1.1 %collective-permute-start.4 = (bf16[128,1024]{1,0:T(8,128)(2,1)S(1)}, bf16[128,1024]{1,0:T(8,128)(2,1)S(1)}, u32[]{:S(2)}, u32[]{:S(2)}) collective-permute-start(bf16[128,1024]{1,0:T(8,128)(2,1)S(1)} %bitcast.32), channel_id=1, source_target_pairs={{0,16},{16,0},{1,17},{17,1},{2,18},{18,2},{3,19},{19,3},{4,20},{20... | collective-permute-start | bytes 786440 | tf_op jit(solution)/shard_map/ppermute | solution.py:442
  61.1 1.2 %collective-permute-done.4.fix_twin_ref = bf16[128,1024]{1,0:T(8,128)(2,1)S(1)} collective-permute-done((bf16[128,1024]{1,0:T(8,128)(2,1)S(1)}, bf16[128,1024]{1,0:T(8,128)(2,1)S(1)}, u32[]{:S(2)}, u32[]{:S(2)}) %collective-permute-start.4) | collective-permute-done | bytes 262176 | tf_op jit(solution)/shard_map/ppermute | solution.py:442
  62.3 2.3 %shard_map.40 = f32[32,8,128]{2,1,0:T(8,128)S(1)} custom-call(s32[4]{0:T(128)S(1)} %pad_add_fusion.ids_ref, f32[8,128]{1,0:T(8,128)S(1)} %get-tuple-element.102.flag_ref, f32[8,1024]{1,0:T(8,128)S(1)} %get-tuple-element.105.rows_ref, f32[1024,128]{1,0:T(8,128)S(1)} %get-tuple-element.106.own_key_ref, f32[16,128]{1,0:T(8,128)S(1)} %get-tuple-element.109.code_ref, ...), custom_call_target="tpu_custom_call" | custom-call | flops 1073741824 | bytes 4194304 | tf_op jit(solution)/shard_map/pallas_call | solution.py:339
  64.7 10.9 %all_to_all.21.in_ref = f32[32,8,128]{2,1,0:T(8,128)S(1)} all-to-all(f32[32,8,128]{2,1,0:T(8,128)S(1)} %shard_map.40), channel_id=1, replica_groups=mesh['x'=4,'core'=2,'yh'=2,'yl'=2,'z'=4] {'core','yh','yl','z'}, dimensions={0} | all-to-all | bytes 262144 | tf_op jit(solution)/shard_map/all_to_all | solution.py:444
  75.5 1.8 %shard_map.41 = (f32[6,128]{1,0:T(8,128)}, s32[1]{0:T(128)}) custom-call(s32[4]{0:T(128)S(1)} %pad_add_fusion.ids_ref, f32[32,8,128]{2,1,0:T(8,128)S(1)} %all_to_all.21.in_ref), custom_call_target="tpu_custom_call" | custom-call | flops 134217728 | bytes 4194304 | tf_op jit(solution)/shard_map/pallas_call | solution.py:339
  77.4 0.8 %while.24 = (s32[]{:T(128)}, f32[768]{0:T(1024)}, bf16[1024,1024]{1,0:T(8,128)(2,1)}, s32[]{:T(128)}, s32[]{:T(128)}, /*index=5*/s32[4]{0:T(128)S(1)}) while((s32[]{:T(128)}, f32[768]{0:T(1024)}, bf16[1024,1024]{1,0:T(8,128)(2,1)}, s32[]{:T(128)}, s32[]{:T(128)}, /*index=5*/s32[4]{0:T(128)S(1)}) %tuple.50), condition=%region_4.5_spmd, body=%region_0.4_spmd | while | flops 2287025152 | bytes 43379448 | solution.py:446
Async XLA Ops:
  44.6 8.7 %collective-permute-start.3 = (bf16[1024,1024]{1,0:T(8,128)(2,1)S(1)}, bf16[1024,1024]{1,0:T(8,128)(2,1)}, u32[]{:S(2)}, u32[]{:S(2)}) collective-permute-start(bf16[1024,1024]{1,0:T(8,128)(2,1)S(1)} %bitcast.27), channel_id=1, source_target_pairs={{0,16},{16,0},{1,17},{17,1},{2,18},{18,2},{3,19},{19,3},{4,20},{20... | collective-permute-start | bytes 6291464 | tf_op jit(solution)/shard_map/ppermute | solution.py:435
  49.9 10.2 %all-to-all-start.2 = ((bf16[8,16,1024]{2,1,0:T(8,128)(2,1)}), bf16[8,16,1024]{2,1,0:T(8,128)(2,1)S(1)}, u32[]{:S(2)}, u32[]{:S(2)}) async-start(bf16[8,16,1024]{2,1,0:T(8,128)(2,1)} %bitcast.6), calls=%async_computation.2 | async-start | bytes 524288 | tf_op jit(solution)/shard_map/all_to_all | solution.py:437
  60.0 2.3 %collective-permute-start.4 = (bf16[128,1024]{1,0:T(8,128)(2,1)S(1)}, bf16[128,1024]{1,0:T(8,128)(2,1)S(1)}, u32[]{:S(2)}, u32[]{:S(2)}) collective-permute-start(bf16[128,1024]{1,0:T(8,128)(2,1)S(1)} %bitcast.32), channel_id=1, source_target_pairs={{0,16},{16,0},{1,17},{17,1},{2,18},{18,2},{3,19},{19,3},{4,20},{20... | collective-permute-start | bytes 786440 | tf_op jit(solution)/shard_map/ppermute | solution.py:442

commit v6 on v5

--- a/solution.py
+++ b/solution.py
@@ -21,7 +21,7 @@
 FIX = LABELS * SLOT
 ALL = ("x", "core", "yh", "yl", "z")
 CHIP_AXES = ("x", "yh", "yl", "z")
-GROUP_CHIPS = ("yl", "z")
+GROUP_CORES = ("core", "yl", "z")
 PLANE = ("core", "yh", "yl", "z")
 NEVER = 1.0e9
 VMEM = 24 * 1024 * 1024
@@ -175,10 +175,12 @@
     for b in range(0, D, 256):
         part = mm(pick, main_ref[:, b:b + 256])
         if b == 0:
-            out_ref[:, 0:128] = jnp.where((iota(fixed, 0) & 15) == CAP, tag, part[:, 0:128]).astype(BF)
-            out_ref[:, 128:256] = part[:, 128:256].astype(BF)
+            part = jnp.concatenate([jnp.where((iota(fixed, 0) & 15) == CAP, tag, part[:, 0:128]), part[:, 128:256]], axis=1)
+            out_ref[0:FIX, 0:256] = part.astype(BF)
+            out_ref[FIX:2 * FIX, 0:256] = part.astype(BF)
         else:
-            out_ref[:, b:b + 256] = part.astype(BF)
+            out_ref[0:FIX, b:b + 256] = part.astype(BF)
+            out_ref[FIX:2 * FIX, b:b + 256] = part.astype(BF)
     worst = jnp.max(jnp.where(moved, rank, 0.0), axis=1, keepdims=True)
     flag_ref[...] = jnp.broadcast_to(jnp.where(worst >= CAP, 1.0, 0.0), (8, 128))
 
@@ -235,13 +237,13 @@
     rows_ref[...] = rows
 
 
-def last_kernel(ids_ref, flag_ref, rows_ref, own_key_ref, code_ref, own_ref, fix_ref, fix_twin_ref, out_ref):
+def last_kernel(ids_ref, flag_ref, rows_ref, own_key_ref, code_ref, own_ref, fix_ref, out_ref):
     core = ids_ref[0]
-    fix_rows = jnp.concatenate([fix_ref[...], fix_twin_ref[...]], axis=0)
+    fix_rows = fix_ref[...]
     tags = tag_rows(fix_rows[:, 0:128], 2 * LABELS)
 
     def side(shape, dim):
-        return core ^ lax.shift_right_logical(iota(shape, dim), 7)
+        return lax.shift_right_logical(iota(shape, dim), 7)
 
     tall, wide = (2 * FIX, 1), (1, 2 * FIX)
     valid, chip, at = tag_columns(tags, 2 * LABELS, (0, 1, 2))
@@ -403,7 +405,7 @@
 
 
 def fix_call(ids, main):
-    shapes = (struct((FIX, D), BF), struct((8, 128), F32), struct((CHIPS, 128), BF), struct((8, MAIN), F32))
+    shapes = (struct((2 * FIX, D), BF), struct((8, 128), F32), struct((CHIPS, 128), BF), struct((8, MAIN), F32))
     return call(fix_kernel, shapes, (ids, main), 1 << 30)
 
 
@@ -435,12 +437,11 @@
     twin = lax.ppermute(main, "core", swap)
     fix, flag, tags, lanes = fix_call(ids, main)
     fix = lax.all_to_all(
-        fix.reshape(LABELS, SLOT, D), GROUP_CHIPS, split_axis=0, concat_axis=0, tiled=True
-    ).reshape(FIX, D)
+        fix.reshape(2 * LABELS, SLOT, D), GROUP_CORES, split_axis=0, concat_axis=0, tiled=True
+    ).reshape(2 * FIX, D)
     parts = main_call(ids, tags, lanes, main, twin)
     fix, code = lax.optimization_barrier((fix, parts[2]))
-    fix_twin = lax.ppermute(fix, "core", swap)
-    table = last_call(ids, flag, *parts[:2], code, main, fix, fix_twin)
+    table = last_call(ids, flag, *parts[:2], code, main, fix)
     back = lax.all_to_all(table, PLANE, split_axis=0, concat_axis=0, tiled=True)
     out, flag = put_call(ids, back)
     _, out = lax.while_loop(

time: 78.7 us -> 80.2 us (1.019)
  waiting for transfers between devices: 2.72 us -> 5.31 us
  starting transfers between devices: 7.47 us -> 6.41 us
    all_to_all x1, waiting for transfers between devices: 1.55 us -> 5.31 us  [body(): lax.all_to_all(fix.reshape(2 * LABELS, SLOT, D), GROUP_CORES, split_axis=...]
    ppermute x1 -> x0, waiting for transfers between devices: 1.16 us -> none  [body(): fix_twin = lax.ppermute(fix, 'core', swap)]
    ppermute x1 -> x0, starting transfers between devices: 1.12 us -> none  [body(): fix_twin = lax.ppermute(fix, 'core', swap)]
  transfers between devices with their start and end apart: 3 -> 2, of which waited for: 2 -> 1; matrix products, arithmetic and copies ran while one was open for 0% -> 0% of each run, Pallas kernels for 10% -> 10%
where the time goes in v6:
time: 80.2 us; the launch traced here: 79.9 us
  blocking collectives  50.2 us (63%)
  Pallas kernels  16.8 us (21%)
  starting transfers between devices  6.41 us (8%)
  waiting for transfers between devices  5.31 us (7%)
  loops' own time  0.82 us (1%)
    all_to_all x1, blocking collectives, body(): lax.all_to_all(packed.reshape(CHIPS, SLOT, D), CHIP_AXES, split_axis=0, c...  39.5 us
    pallas_call x5, Pallas kernels, call(): pl.pallas_call(kernel, out_shape=shapes, in_specs=specs, out_specs=out_sp...  16.8 us
    all_to_all x1, blocking collectives, body(): back = lax.all_to_all(table, PLANE, split_axis=0, concat_axis=0, tiled=True)  10.8 us
    all_to_all x1, waiting for transfers between devices, body(): lax.all_to_all(fix.reshape(2 * LABELS, SLOT, D), GROUP_CORES, split_axis=...  5.31 us
    all_to_all x1, starting transfers between devices, body(): lax.all_to_all(fix.reshape(2 * LABELS, SLOT, D), GROUP_CORES, split_axis=...  3.47 us
    ppermute x1, starting transfers between devices, body(): twin = lax.ppermute(main, 'core', swap)  2.94 us
  transfers between devices with their start and end apart: 2, of which 1 were waited for; matrix products, arithmetic and copies ran while one was open for 0% of the time, Pallas kernels for 10%

profile of v6, /device:TPU:1, one launch (start us, length us, event | category | flops | bytes accessed | tf_op | source)
XLA Modules:
  0.0 79.9 jit_solution(7083245992292597392)
XLA Ops:
  0.0 0.1 pad_add_fusion.ids_ref
  0.1 5.0 %shard_map.37 = bf16[1024,1024]{1,0:T(8,128)(2,1)S(1)} custom-call(s32[4]{0:T(128)S(1)} %pad_add_fusion.ids_ref, bf16[768,1024]{1,0:T(8,128)(2,1)} %emb_hbm.1, s32[768]{0:T(1024)} %lab_hbm.1, s32[1,768]{1,0:T(1,128)} %list_hbm.1), custom_call_target="tpu_custom_call" | custom-call | flops 3221225472 | bytes 4194304 | tf_op jit(solution)/shard_map/pallas_call | solution.py:341
  5.1 39.5 %all_to_all.20 = bf16[64,16,1024]{2,1,0:T(8,128)(2,1)S(1)} all-to-all(bf16[64,16,1024]{2,1,0:T(8,128)(2,1)S(1)} %bitcast.31), channel_id=1, replica_groups=mesh['x'=4,'core'=2,'yh'=2,'yl'=2,'z'=4] {'x','yh','yl','z'}, dimensions={0} | all-to-all | bytes 4194304 | tf_op jit(solution)/shard_map/all_to_all | solution.py:433
  44.6 2.9 %collective-permute-start.3 = (bf16[1024,1024]{1,0:T(8,128)(2,1)S(1)}, bf16[1024,1024]{1,0:T(8,128)(2,1)}, u32[]{:S(2)}, u32[]{:S(2)}) collective-permute-start(bf16[1024,1024]{1,0:T(8,128)(2,1)S(1)} %bitcast.27), channel_id=1, source_target_pairs={{0,16},{16,0},{1,17},{17,1},{2,18},{18,2},{3,19},{19,3},{4,20},{20... | collective-permute-start | bytes 6291464 | tf_op jit(solution)/shard_map/ppermute | solution.py:437
  47.5 2.5 %shard_map.38 = (bf16[256,1024]{1,0:T(8,128)(2,1)}, f32[8,128]{1,0:T(8,128)S(1)}, bf16[64,128]{1,0:T(8,128)(2,1)S(1)}, f32[8,1024]{1,0:T(8,128)S(1)}) custom-call(s32[4]{0:T(128)S(1)} %pad_add_fusion.ids_ref, bf16[1024,1024]{1,0:T(8,128)(2,1)S(1)} %bitcast.28), custom_call_target="tpu_custom_call" | custom-call | flops 1073741824 | bytes 4194304 | tf_op jit(solution)/shard_map/pallas_call | solution.py:341
  50.0 3.5 %all-to-all-start.2 = ((bf16[16,16,1024]{2,1,0:T(8,128)(2,1)}), bf16[16,16,1024]{2,1,0:T(8,128)(2,1)S(1)}, u32[]{:S(2)}, u32[]{:S(2)}) async-start(bf16[16,16,1024]{2,1,0:T(8,128)(2,1)} %bitcast.6), calls=%async_computation.2 | async-start | bytes 1048576 | tf_op jit(solution)/shard_map/all_to_all | solution.py:439
  53.5 0.0 collective-permute-done.3.twin_ref
  53.5 5.2 %shard_map.39 = (f32[8,1024]{1,0:T(8,128)S(1)}, f32[1024,128]{1,0:T(8,128)S(1)}, f32[16,128]{1,0:T(8,128)S(1)}) custom-call(s32[4]{0:T(128)S(1)} %pad_add_fusion.ids_ref, bf16[64,128]{1,0:T(8,128)(2,1)S(1)} %get-tuple-element.103.tags_ref, f32[8,1024]{1,0:T(8,128)S(1)} %get-tuple-element.104.lanes_ref, bf16[1024,1024]{1,0:T(8,128)(2,1)S(1)} %bitcast.29, ...), custom_call_target="tpu_custom_call" | custom-call | flops 3221225472 | bytes 4194304 | tf_op jit(solution)/shard_map/pallas_call | solution.py:341
  58.6 5.3 %all-to-all-done.2 = bf16[16,16,1024]{2,1,0:T(8,128)(2,1)S(1)} async-done(((bf16[16,16,1024]{2,1,0:T(8,128)(2,1)}), bf16[16,16,1024]{2,1,0:T(8,128)(2,1)S(1)}, u32[]{:S(2)}, u32[]{:S(2)}) %all-to-all-start.2) | async-done | bytes 524320 | tf_op jit(solution)/shard_map/all_to_all | solution.py:439
  63.9 2.3 %shard_map.40 = f32[32,8,128]{2,1,0:T(8,128)S(1)} custom-call(s32[4]{0:T(128)S(1)} %pad_add_fusion.ids_ref, f32[8,128]{1,0:T(8,128)S(1)} %get-tuple-element.102.flag_ref, f32[8,1024]{1,0:T(8,128)S(1)} %get-tuple-element.105.rows_ref, f32[1024,128]{1,0:T(8,128)S(1)} %get-tuple-element.106.own_key_ref, f32[16,128]{1,0:T(8,128)S(1)} %get-tuple-element.109.code_ref, ...), custom_call_target="tpu_custom_call" | custom-call | flops 1073741824 | bytes 4194304 | tf_op jit(solution)/shard_map/pallas_call | solution.py:341
  66.3 10.8 %all_to_all.21.in_ref = f32[32,8,128]{2,1,0:T(8,128)S(1)} all-to-all(f32[32,8,128]{2,1,0:T(8,128)S(1)} %shard_map.40), channel_id=1, replica_groups=mesh['x'=4,'core'=2,'yh'=2,'yl'=2,'z'=4] {'core','yh','yl','z'}, dimensions={0} | all-to-all | bytes 262144 | tf_op jit(solution)/shard_map/all_to_all | solution.py:445
  77.1 1.8 %shard_map.41 = (f32[6,128]{1,0:T(8,128)}, s32[1]{0:T(128)}) custom-call(s32[4]{0:T(128)S(1)} %pad_add_fusion.ids_ref, f32[32,8,128]{2,1,0:T(8,128)S(1)} %all_to_all.21.in_ref), custom_call_target="tpu_custom_call" | custom-call | flops 134217728 | bytes 4194304 | tf_op jit(solution)/shard_map/pallas_call | solution.py:341
  78.9 0.8 %while.24 = (s32[]{:T(128)}, f32[768]{0:T(1024)}, bf16[1024,1024]{1,0:T(8,128)(2,1)}, s32[]{:T(128)}, s32[]{:T(128)}, /*index=5*/s32[4]{0:T(128)S(1)}) while((s32[]{:T(128)}, f32[768]{0:T(1024)}, bf16[1024,1024]{1,0:T(8,128)(2,1)}, s32[]{:T(128)}, s32[]{:T(128)}, /*index=5*/s32[4]{0:T(128)S(1)}) %tuple.50), condition=%region_4.5_spmd, body=%region_0.4_spmd | while | flops 2287025152 | bytes 43379448 | solution.py:447
Async XLA Ops:
  44.6 8.9 %collective-permute-start.3 = (bf16[1024,1024]{1,0:T(8,128)(2,1)S(1)}, bf16[1024,1024]{1,0:T(8,128)(2,1)}, u32[]{:S(2)}, u32[]{:S(2)}) collective-permute-start(bf16[1024,1024]{1,0:T(8,128)(2,1)S(1)} %bitcast.27), channel_id=1, source_target_pairs={{0,16},{16,0},{1,17},{17,1},{2,18},{18,2},{3,19},{19,3},{4,20},{20... | collective-permute-start | bytes 6291464 | tf_op jit(solution)/shard_map/ppermute | solution.py:437
  50.0 14.0 %all-to-all-start.2 = ((bf16[16,16,1024]{2,1,0:T(8,128)(2,1)}), bf16[16,16,1024]{2,1,0:T(8,128)(2,1)S(1)}, u32[]{:S(2)}, u32[]{:S(2)}) async-start(bf16[16,16,1024]{2,1,0:T(8,128)(2,1)} %bitcast.6), calls=%async_computation.2 | async-start | bytes 1048576 | tf_op jit(solution)/shard_map/all_to_all | solution.py:439

commit v7 on v5

--- a/solution.py
+++ b/solution.py
@@ -152,7 +152,7 @@
     return away_order(source_of(chip, core), (holder - chip) & 7, at.astype(I32))
 
 
-def fix_kernel(ids_ref, main_ref, out_ref, flag_ref, tags_ref, lanes_ref):
+def fix_kernel(ids_ref, main_ref, out_hbm, flag_ref, tags_ref, lanes_ref, out_ref, sems):
     own = ids_ref[1].astype(F32)
     tags = tag_rows(main_ref[:, 0:128], CHIPS)
     label = tag_lanes(tags, CHIPS, 0)
@@ -172,15 +172,20 @@
     fixed = (FIX, 128)
     tag = jnp.where((iota(fixed, 1) & 15) == (iota(fixed, 0) & 15), mm_t(pick, vals), 0.0)
     tag = jnp.broadcast_to(jnp.sum(tag.reshape(LABELS, SLOT, 128), axis=1, keepdims=True), (LABELS, SLOT, 128)).reshape(fixed)
-    for b in range(0, D, 256):
+    copies = []
+    for i, b in enumerate(range(0, D, 256)):
         part = mm(pick, main_ref[:, b:b + 256])
         if b == 0:
             out_ref[:, 0:128] = jnp.where((iota(fixed, 0) & 15) == CAP, tag, part[:, 0:128]).astype(BF)
             out_ref[:, 128:256] = part[:, 128:256].astype(BF)
         else:
             out_ref[:, b:b + 256] = part.astype(BF)
+        copies.append(pltpu.make_async_copy(out_ref.at[:, b:b + 256], out_hbm.at[:, b:b + 256], sems.at[i]))
+        copies[-1].start()
     worst = jnp.max(jnp.where(moved, rank, 0.0), axis=1, keepdims=True)
     flag_ref[...] = jnp.broadcast_to(jnp.where(worst >= CAP, 1.0, 0.0), (8, 128))
+    for copy in copies:
+        copy.wait()
 
 
 def lanes_to_rows(row):
@@ -195,42 +200,51 @@
     return found
 
 
-def main_kernel(ids_ref, tags_ref, lanes_ref, own_ref, twin_ref, rows_ref, own_key_ref, code_ref):
+def main_kernel(ids_ref, tags_ref, lanes_ref, own_ref, twin_hbm, rows_ref, own_key_ref, code_ref, twin_ref, sems):
+    fetch = [
+        pltpu.make_async_copy(twin_hbm.at[r:r + 256], twin_ref.at[r:r + 256], sems.at[i])
+        for i, r in enumerate(range(0, MAIN, 256))
+    ]
+    for copy in fetch:
+        copy.start()
     core = ids_ref[0]
     mine = ids_ref[1].astype(F32) + 1.0
-    twin_tags = tag_rows(twin_ref[:, 0:128], CHIPS)
 
     def main_key(t, c):
         (label,) = tag_columns(t, CHIPS, (0,))
         return jnp.broadcast_to(jnp.where(label == mine, main_order((MAIN, 1), 0, c), NEVER), (MAIN, 128))
 
     own_key_ref[...] = main_key(tags_ref[...], core)
-    twin_key = main_key(twin_tags, 1 - core)
     valid = lanes_ref[0:1, :] == mine
     query = jnp.where(valid, main_order((1, MAIN), 1, core), -1.0)
+
+    def score(ref, key, q):
+        return best(((ref[0:q + 256, :], key[0:q + 256, :]),), own_ref[q:q + 256, :], query[:, q:q + 256])
+
+    found = [score(own_ref, own_key_ref, 0), score(own_ref, own_key_ref, 256)]
     dest = lanes_ref[1:2, :].astype(I32)
     home = lax.shift_right_logical(dest * 43, 8)
     member = valid & (iota((16, MAIN), 0) == home)
     ranks = earlier(jnp.where(member, 1.0, 0.0))
+    found.append(score(own_ref, own_key_ref, 512))
     rank = jnp.sum(jnp.where(member, ranks, 0.0), axis=0, keepdims=True)
     rank = jnp.where(valid, rank, -1.0)
+    found.append(score(own_ref, own_key_ref, 768))
     hot = onehot(iota((128, MAIN), 0).astype(F32) == rank)
     source = source_of(lax.shift_right_logical(iota((1, MAIN), 1), 4), core)
     at = source * 6 + dest - home * 6 + 1
     high = lax.shift_right_logical(at, 4)
     parts = [jnp.where(member, part.astype(F32), 0.0).astype(BF) for part in (high, at - high * 16)]
+    for copy in fetch:
+        copy.wait()
+    twin_key = main_key(tag_rows(twin_ref[:, 0:128], CHIPS), 1 - core)
+    found[0] = jnp.maximum(found[0], score(twin_ref, twin_key, 0))
+    found[1] = jnp.maximum(found[1], score(twin_ref, twin_key, 256))
     code_ref[...] = mm_t(parts[0], hot) * 16.0 + mm_t(parts[1], hot) - 1.0
-    worst = jnp.max(rank, axis=1, keepdims=True)
-    found = [
-        best(
-            ((own_ref[0:q + 256, :], own_key_ref[0:q + 256, :]), (twin_ref[0:q + 256, :], twin_key[0:q + 256, :])),
-            own_ref[q:q + 256, :],
-            query[:, q:q + 256],
-        )
-        for q in range(0, MAIN, 256)
-    ]
+    found[2] = jnp.maximum(found[2], score(twin_ref, twin_key, 512))
+    found[3] = jnp.maximum(found[3], score(twin_ref, twin_key, 768))
+    worst = jnp.broadcast_to(jnp.max(rank, axis=1, keepdims=True), (1, MAIN))
     found = jnp.concatenate(found, axis=1)
-    worst = jnp.broadcast_to(worst, (1, MAIN))
     rows = jnp.concatenate([query, found, home.astype(F32), worst, rank, jnp.zeros((3, MAIN), F32)], axis=0)
     rows_ref[...] = rows
 
@@ -335,7 +349,8 @@
 
 
 def call(kernel, shapes, args, flops, memory=pltpu.VMEM, scratch=(), vmem=VMEM, out_memory=pltpu.VMEM, out_specs=None):
-    specs = [pl.BlockSpec(memory_space=pltpu.SMEM)] + [pl.BlockSpec(memory_space=memory)] * (len(args) - 1)
+    memory = memory if isinstance(memory, list) else [memory] * (len(args) - 1)
+    specs = [pl.BlockSpec(memory_space=space) for space in [pltpu.SMEM] + memory]
     return pl.pallas_call(
         kernel,
         out_shape=shapes,
@@ -404,13 +419,17 @@
 
 def fix_call(ids, main):
     shapes = (struct((FIX, D), BF), struct((8, 128), F32), struct((CHIPS, 128), BF), struct((8, MAIN), F32))
-    return call(fix_kernel, shapes, (ids, main), 1 << 30)
+    specs = tuple(pl.BlockSpec(memory_space=space) for space in (pltpu.HBM,) + (pltpu.VMEM,) * 3)
+    scratch = (pltpu.VMEM((FIX, D), BF), pltpu.SemaphoreType.DMA((4,)))
+    return call(fix_kernel, shapes, (ids, main), 1 << 30, scratch=scratch, out_specs=specs)
 
 
 def main_call(*args):
     wide = struct((MAIN, 128), F32)
     shapes = (struct((8, MAIN), F32), wide, struct((16, 128), F32))
-    return call(main_kernel, shapes, args, 3 << 30)
+    memory = [pltpu.VMEM] * 3 + [pl.ANY]
+    scratch = (pltpu.VMEM((MAIN, D), BF), pltpu.SemaphoreType.DMA((4,)))
+    return call(main_kernel, shapes, args, 3 << 30, memory, scratch)
 
 
 def last_call(*args):

time: 78.7 us -> 78.6 us (level)
  transfers between devices with their start and end apart: 3 -> 3, of which waited for: 2 -> 2; matrix products, arithmetic and copies ran while one was open for 0% -> 0% of each run, Pallas kernels for 10% -> 9%
where the time goes in v7:
time: 78.6 us; the launch traced here: 78.3 us
  blocking collectives  50.3 us (64%)
  Pallas kernels  16.4 us (21%)
  starting transfers between devices  7.5 us (10%)
  waiting for transfers between devices  2.93 us (4%)
  loops' own time  0.81 us (1%)
    all_to_all x1, blocking collectives, body(): lax.all_to_all(packed.reshape(CHIPS, SLOT, D), CHIP_AXES, split_axis=0, c...  39.5 us
    pallas_call x5, Pallas kernels, call(): pl.pallas_call(kernel, out_shape=shapes, in_specs=specs, out_specs=out_sp...  16.4 us
    all_to_all x1, blocking collectives, body(): back = lax.all_to_all(table, PLANE, split_axis=0, concat_axis=0, tiled=True)  10.9 us
    all_to_all x1, starting transfers between devices, body(): lax.all_to_all(fix.reshape(LABELS, SLOT, D), GROUP_CHIPS, split_axis=0, c...  3.42 us
    ppermute x1, starting transfers between devices, body(): twin = lax.ppermute(main, 'core', swap)  2.94 us
    all_to_all x1, waiting for transfers between devices, body(): lax.all_to_all(fix.reshape(LABELS, SLOT, D), GROUP_CHIPS, split_axis=0, c...  1.76 us
  transfers between devices with their start and end apart: 3, of which 2 were waited for; matrix products, arithmetic and copies ran while one was open for 0% of the time, Pallas kernels for 9%

profile of v7, /device:TPU:1, one launch (start us, length us, event | category | flops | bytes accessed | tf_op | source)
XLA Modules:
  0.0 78.3 jit_solution(11135168872149198474)
XLA Ops:
  0.0 0.1 pad_add_fusion.ids_ref
  0.1 5.0 %shard_map.37 = bf16[1024,1024]{1,0:T(8,128)(2,1)S(1)} custom-call(s32[4]{0:T(128)S(1)} %pad_add_fusion.ids_ref, bf16[768,1024]{1,0:T(8,128)(2,1)} %emb_hbm.1, s32[768]{0:T(1024)} %lab_hbm.1, s32[1,768]{1,0:T(1,128)} %list_hbm.1), custom_call_target="tpu_custom_call" | custom-call | flops 3221225472 | bytes 4194304 | tf_op jit(solution)/shard_map/pallas_call | solution.py:354
  5.1 39.5 %all_to_all.20 = bf16[64,16,1024]{2,1,0:T(8,128)(2,1)S(1)} all-to-all(bf16[64,16,1024]{2,1,0:T(8,128)(2,1)S(1)} %bitcast.31), channel_id=1, replica_groups=mesh['x'=4,'core'=2,'yh'=2,'yl'=2,'z'=4] {'x','yh','yl','z'}, dimensions={0} | all-to-all | bytes 4194304 | tf_op jit(solution)/shard_map/all_to_all | solution.py:450
  44.6 2.9 %collective-permute-start.3 = (bf16[1024,1024]{1,0:T(8,128)(2,1)S(1)}, bf16[1024,1024]{1,0:T(8,128)(2,1)}, u32[]{:S(2)}, u32[]{:S(2)}) collective-permute-start(bf16[1024,1024]{1,0:T(8,128)(2,1)S(1)} %bitcast.27), channel_id=1, source_target_pairs={{0,16},{16,0},{1,17},{17,1},{2,18},{18,2},{3,19},{19,3},{4,20},{20... | collective-permute-start | bytes 6291464 | tf_op jit(solution)/shard_map/ppermute | solution.py:454
  47.5 2.3 %shard_map.38 = (bf16[128,1024]{1,0:T(8,128)(2,1)}, f32[8,128]{1,0:T(8,128)S(1)}, bf16[64,128]{1,0:T(8,128)(2,1)S(1)}, f32[8,1024]{1,0:T(8,128)S(1)}) custom-call(s32[4]{0:T(128)S(1)} %pad_add_fusion.ids_ref, bf16[1024,1024]{1,0:T(8,128)(2,1)S(1)} %bitcast.28), custom_call_target="tpu_custom_call" | custom-call | flops 1073741824 | bytes 4194304 | tf_op jit(solution)/shard_map/pallas_call | solution.py:354
  49.8 3.4 %all-to-all-start.2 = ((bf16[8,16,1024]{2,1,0:T(8,128)(2,1)}), bf16[8,16,1024]{2,1,0:T(8,128)(2,1)S(1)}, u32[]{:S(2)}, u32[]{:S(2)}) async-start(bf16[8,16,1024]{2,1,0:T(8,128)(2,1)} %bitcast.6), calls=%async_computation.2 | async-start | bytes 524288 | tf_op jit(solution)/shard_map/all_to_all | solution.py:456
  53.3 0.0 collective-permute-done.3.twin_hbm
  53.3 4.9 %shard_map.39 = (f32[8,1024]{1,0:T(8,128)S(1)}, f32[1024,128]{1,0:T(8,128)S(1)}, f32[16,128]{1,0:T(8,128)S(1)}) custom-call(s32[4]{0:T(128)S(1)} %pad_add_fusion.ids_ref, bf16[64,128]{1,0:T(8,128)(2,1)S(1)} %get-tuple-element.103.tags_ref, f32[8,1024]{1,0:T(8,128)S(1)} %get-tuple-element.104.lanes_ref, bf16[1024,1024]{1,0:T(8,128)(2,1)S(1)} %bitcast.29, ...), custom_call_target="tpu_custom_call" | custom-call | flops 3221225472 | bytes 4194304 | tf_op jit(solution)/shard_map/pallas_call | solution.py:354
  58.2 1.8 %all-to-all-done.2 = bf16[8,16,1024]{2,1,0:T(8,128)(2,1)S(1)} async-done(((bf16[8,16,1024]{2,1,0:T(8,128)(2,1)}), bf16[8,16,1024]{2,1,0:T(8,128)(2,1)S(1)}, u32[]{:S(2)}, u32[]{:S(2)}) %all-to-all-start.2) | async-done | bytes 262176 | tf_op jit(solution)/shard_map/all_to_all | solution.py:456
  60.0 1.1 %collective-permute-start.4 = (bf16[128,1024]{1,0:T(8,128)(2,1)S(1)}, bf16[128,1024]{1,0:T(8,128)(2,1)S(1)}, u32[]{:S(2)}, u32[]{:S(2)}) collective-permute-start(bf16[128,1024]{1,0:T(8,128)(2,1)S(1)} %bitcast.32), channel_id=1, source_target_pairs={{0,16},{16,0},{1,17},{17,1},{2,18},{18,2},{3,19},{19,3},{4,20},{20... | collective-permute-start | bytes 786440 | tf_op jit(solution)/shard_map/ppermute | solution.py:461
  61.1 1.2 %collective-permute-done.4.fix_twin_ref = bf16[128,1024]{1,0:T(8,128)(2,1)S(1)} collective-permute-done((bf16[128,1024]{1,0:T(8,128)(2,1)S(1)}, bf16[128,1024]{1,0:T(8,128)(2,1)S(1)}, u32[]{:S(2)}, u32[]{:S(2)}) %collective-permute-start.4) | collective-permute-done | bytes 262176 | tf_op jit(solution)/shard_map/ppermute | solution.py:461
  62.3 2.3 %shard_map.40 = f32[32,8,128]{2,1,0:T(8,128)S(1)} custom-call(s32[4]{0:T(128)S(1)} %pad_add_fusion.ids_ref, f32[8,128]{1,0:T(8,128)S(1)} %get-tuple-element.102.flag_ref, f32[8,1024]{1,0:T(8,128)S(1)} %get-tuple-element.105.rows_ref, f32[1024,128]{1,0:T(8,128)S(1)} %get-tuple-element.106.own_key_ref, f32[16,128]{1,0:T(8,128)S(1)} %get-tuple-element.109.code_ref, ...), custom_call_target="tpu_custom_call" | custom-call | flops 1073741824 | bytes 4194304 | tf_op jit(solution)/shard_map/pallas_call | solution.py:354
  64.6 10.9 %all_to_all.21.in_ref = f32[32,8,128]{2,1,0:T(8,128)S(1)} all-to-all(f32[32,8,128]{2,1,0:T(8,128)S(1)} %shard_map.40), channel_id=1, replica_groups=mesh['x'=4,'core'=2,'yh'=2,'yl'=2,'z'=4] {'core','yh','yl','z'}, dimensions={0} | all-to-all | bytes 262144 | tf_op jit(solution)/shard_map/all_to_all | solution.py:463
  75.5 1.8 %shard_map.41 = (f32[6,128]{1,0:T(8,128)}, s32[1]{0:T(128)}) custom-call(s32[4]{0:T(128)S(1)} %pad_add_fusion.ids_ref, f32[32,8,128]{2,1,0:T(8,128)S(1)} %all_to_all.21.in_ref), custom_call_target="tpu_custom_call" | custom-call | flops 134217728 | bytes 4194304 | tf_op jit(solution)/shard_map/pallas_call | solution.py:354
  77.3 0.8 %while.24 = (s32[]{:T(128)}, f32[768]{0:T(1024)}, bf16[1024,1024]{1,0:T(8,128)(2,1)}, s32[]{:T(128)}, s32[]{:T(128)}, /*index=5*/s32[4]{0:T(128)S(1)}) while((s32[]{:T(128)}, f32[768]{0:T(1024)}, bf16[1024,1024]{1,0:T(8,128)(2,1)}, s32[]{:T(128)}, s32[]{:T(128)}, /*index=5*/s32[4]{0:T(128)S(1)}) %tuple.50), condition=%region_4.5_spmd, body=%region_0.4_spmd | while | flops 2287025152 | bytes 43379448 | solution.py:465
Async XLA Ops:
  44.6 8.7 %collective-permute-start.3 = (bf16[1024,1024]{1,0:T(8,128)(2,1)S(1)}, bf16[1024,1024]{1,0:T(8,128)(2,1)}, u32[]{:S(2)}, u32[]{:S(2)}) collective-permute-start(bf16[1024,1024]{1,0:T(8,128)(2,1)S(1)} %bitcast.27), channel_id=1, source_target_pairs={{0,16},{16,0},{1,17},{17,1},{2,18},{18,2},{3,19},{19,3},{4,20},{20... | collective-permute-start | bytes 6291464 | tf_op jit(solution)/shard_map/ppermute | solution.py:454
  49.8 10.2 %all-to-all-start.2 = ((bf16[8,16,1024]{2,1,0:T(8,128)(2,1)}), bf16[8,16,1024]{2,1,0:T(8,128)(2,1)S(1)}, u32[]{:S(2)}, u32[]{:S(2)}) async-start(bf16[8,16,1024]{2,1,0:T(8,128)(2,1)} %bitcast.6), calls=%async_computation.2 | async-start | bytes 524288 | tf_op jit(solution)/shard_map/all_to_all | solution.py:456
  60.0 2.3 %collective-permute-start.4 = (bf16[128,1024]{1,0:T(8,128)(2,1)S(1)}, bf16[128,1024]{1,0:T(8,128)(2,1)S(1)}, u32[]{:S(2)}, u32[]{:S(2)}) collective-permute-start(bf16[128,1024]{1,0:T(8,128)(2,1)S(1)} %bitcast.32), channel_id=1, source_target_pairs={{0,16},{16,0},{1,17},{17,1},{2,18},{18,2},{3,19},{19,3},{4,20},{20... | collective-permute-start | bytes 786440 | tf_op jit(solution)/shard_map/ppermute | solution.py:461

commit v8 on v7

--- a/solution.py
+++ b/solution.py
@@ -63,20 +63,24 @@
     for copy in copies:
         copy.start()
     rot = ids_ref[2]
-    copies[0].wait()
-    copies[1].wait()
-    listed = onehot(iota((ROWS, ROWS), 0) == list_ref[...])
+    before = onehot(iota((ROWS, ROWS), 0) < iota((ROWS, ROWS), 1))
     pos = iota((16, ROWS), 1)
     group_of = lax.shift_right_logical(pos * 683, 16)
     sel = iota((16, ROWS), 0)
     vals = jnp.where(sel == 0, group_of, jnp.where(sel == 1, pos - group_of * 96, 0)).astype(F32).astype(BF)
+    slot = iota((MAIN, 128), 0)
+    at = (slot & 15).astype(F32)
+    chip_hot = onehot(lax.shift_right_logical(iota((MAIN, CHIPS), 0), 4) == iota((MAIN, CHIPS), 1))
+    copies[0].wait()
+    copies[1].wait()
+    listed = onehot(iota((ROWS, ROWS), 0) == list_ref[...])
     gd = mm_t(vals, listed)
     group = gd[0:1]
     dest = gd[1:2]
     label = lab_ref[...].reshape(1, ROWS).astype(F32)
     cluster = group * 8.0 + label
     member = iota((CHIPS, ROWS), 0).astype(F32) == cluster
-    ranks = earlier(jnp.where(member, 1.0, 0.0))
+    ranks = mm(onehot(member), before)
     rank = jnp.sum(jnp.where(member, ranks, 0.0), axis=0, keepdims=True)
     count = jnp.broadcast_to(jnp.sum(jnp.where(member, 1.0, 0.0), axis=1, keepdims=True), (CHIPS, 128))
     over = jnp.maximum(count - CAP, 0.0).astype(BF)
@@ -90,9 +94,6 @@
     free_pre = mm(onehot(same), higher) + mm(onehot(same & (((c1 - rot) & 7) < ((c0 - rot) & 7))), level)
     over_at = jnp.sum(jnp.where(member, over_pre[:, 0:1], 0.0), axis=0, keepdims=True) + rank - CAP
     row_code = jnp.where(rank < CAP, cluster * 16.0 + rank, 2048.0 + group * 128.0 + over_at)
-    slot = iota((MAIN, 128), 0)
-    at = (slot & 15).astype(F32)
-    chip_hot = onehot(lax.shift_right_logical(iota((MAIN, CHIPS), 0), 4) == iota((MAIN, CHIPS), 1))
     slot_count = mm(chip_hot, count.astype(BF))
     slot_free = jnp.where(iota((MAIN, 128), 1) == (slot & 15), mm(chip_hot, free_pre.astype(BF)), 0.0)
     slot_free = jnp.sum(slot_free, axis=1, keepdims=True)

time: 78.6 us -> 78.6 us (level)
  no operation moved by 1% of the time
where the time goes in v8:
time: 78.6 us; the launch traced here: 78.3 us
  blocking collectives  50.3 us (64%)
  Pallas kernels  16.4 us (21%)
  starting transfers between devices  7.57 us (10%)
  waiting for transfers between devices  2.93 us (4%)
  loops' own time  0.81 us (1%)
    all_to_all x1, blocking collectives, body(): lax.all_to_all(packed.reshape(CHIPS, SLOT, D), CHIP_AXES, split_axis=0, c...  39.4 us
    pallas_call x5, Pallas kernels, call(): pl.pallas_call(kernel, out_shape=shapes, in_specs=specs, out_specs=out_sp...  16.4 us
    all_to_all x1, blocking collectives, body(): back = lax.all_to_all(table, PLANE, split_axis=0, concat_axis=0, tiled=True)  10.9 us
    all_to_all x1, starting transfers between devices, body(): lax.all_to_all(fix.reshape(LABELS, SLOT, D), GROUP_CHIPS, split_axis=0, c...  3.42 us
    ppermute x1, starting transfers between devices, body(): twin = lax.ppermute(main, 'core', swap)  3.01 us
    all_to_all x1, waiting for transfers between devices, body(): lax.all_to_all(fix.reshape(LABELS, SLOT, D), GROUP_CHIPS, split_axis=0, c...  1.77 us
  transfers between devices with their start and end apart: 3, of which 2 were waited for; matrix products, arithmetic and copies ran while one was open for 0% of the time, Pallas kernels for 9%

profile of v8, /device:TPU:1, one launch (start us, length us, event | category | flops | bytes accessed | tf_op | source)
XLA Modules:
  0.0 78.3 jit_solution(1367719258411261799)
XLA Ops:
  0.0 0.1 pad_add_fusion.ids_ref
  0.1 5.0 %shard_map.37 = bf16[1024,1024]{1,0:T(8,128)(2,1)S(1)} custom-call(s32[4]{0:T(128)S(1)} %pad_add_fusion.ids_ref, bf16[768,1024]{1,0:T(8,128)(2,1)} %emb_hbm.1, s32[768]{0:T(1024)} %lab_hbm.1, s32[1,768]{1,0:T(1,128)} %list_hbm.1), custom_call_target="tpu_custom_call" | custom-call | flops 3221225472 | bytes 4194304 | tf_op jit(solution)/shard_map/pallas_call | solution.py:355
  5.1 39.4 %all_to_all.20 = bf16[64,16,1024]{2,1,0:T(8,128)(2,1)S(1)} all-to-all(bf16[64,16,1024]{2,1,0:T(8,128)(2,1)S(1)} %bitcast.31), channel_id=1, replica_groups=mesh['x'=4,'core'=2,'yh'=2,'yl'=2,'z'=4] {'x','yh','yl','z'}, dimensions={0} | all-to-all | bytes 4194304 | tf_op jit(solution)/shard_map/all_to_all | solution.py:451
  44.5 3.0 %collective-permute-start.3 = (bf16[1024,1024]{1,0:T(8,128)(2,1)S(1)}, bf16[1024,1024]{1,0:T(8,128)(2,1)}, u32[]{:S(2)}, u32[]{:S(2)}) collective-permute-start(bf16[1024,1024]{1,0:T(8,128)(2,1)S(1)} %bitcast.27), channel_id=1, source_target_pairs={{0,16},{16,0},{1,17},{17,1},{2,18},{18,2},{3,19},{19,3},{4,20},{20... | collective-permute-start | bytes 6291464 | tf_op jit(solution)/shard_map/ppermute | solution.py:455
  47.5 2.3 %shard_map.38 = (bf16[128,1024]{1,0:T(8,128)(2,1)}, f32[8,128]{1,0:T(8,128)S(1)}, bf16[64,128]{1,0:T(8,128)(2,1)S(1)}, f32[8,1024]{1,0:T(8,128)S(1)}) custom-call(s32[4]{0:T(128)S(1)} %pad_add_fusion.ids_ref, bf16[1024,1024]{1,0:T(8,128)(2,1)S(1)} %bitcast.28), custom_call_target="tpu_custom_call" | custom-call | flops 1073741824 | bytes 4194304 | tf_op jit(solution)/shard_map/pallas_call | solution.py:355
  49.8 3.4 %all-to-all-start.2 = ((bf16[8,16,1024]{2,1,0:T(8,128)(2,1)}), bf16[8,16,1024]{2,1,0:T(8,128)(2,1)S(1)}, u32[]{:S(2)}, u32[]{:S(2)}) async-start(bf16[8,16,1024]{2,1,0:T(8,128)(2,1)} %bitcast.6), calls=%async_computation.2 | async-start | bytes 524288 | tf_op jit(solution)/shard_map/all_to_all | solution.py:457
  53.2 0.0 collective-permute-done.3.twin_hbm
  53.3 4.9 %shard_map.39 = (f32[8,1024]{1,0:T(8,128)S(1)}, f32[1024,128]{1,0:T(8,128)S(1)}, f32[16,128]{1,0:T(8,128)S(1)}) custom-call(s32[4]{0:T(128)S(1)} %pad_add_fusion.ids_ref, bf16[64,128]{1,0:T(8,128)(2,1)S(1)} %get-tuple-element.103.tags_ref, f32[8,1024]{1,0:T(8,128)S(1)} %get-tuple-element.104.lanes_ref, bf16[1024,1024]{1,0:T(8,128)(2,1)S(1)} %bitcast.29, ...), custom_call_target="tpu_custom_call" | custom-call | flops 3221225472 | bytes 4194304 | tf_op jit(solution)/shard_map/pallas_call | solution.py:355
  58.2 1.8 %all-to-all-done.2 = bf16[8,16,1024]{2,1,0:T(8,128)(2,1)S(1)} async-done(((bf16[8,16,1024]{2,1,0:T(8,128)(2,1)}), bf16[8,16,1024]{2,1,0:T(8,128)(2,1)S(1)}, u32[]{:S(2)}, u32[]{:S(2)}) %all-to-all-start.2) | async-done | bytes 262176 | tf_op jit(solution)/shard_map/all_to_all | solution.py:457
  60.0 1.1 %collective-permute-start.4 = (bf16[128,1024]{1,0:T(8,128)(2,1)S(1)}, bf16[128,1024]{1,0:T(8,128)(2,1)S(1)}, u32[]{:S(2)}, u32[]{:S(2)}) collective-permute-start(bf16[128,1024]{1,0:T(8,128)(2,1)S(1)} %bitcast.32), channel_id=1, source_target_pairs={{0,16},{16,0},{1,17},{17,1},{2,18},{18,2},{3,19},{19,3},{4,20},{20... | collective-permute-start | bytes 786440 | tf_op jit(solution)/shard_map/ppermute | solution.py:462
  61.1 1.2 %collective-permute-done.4.fix_twin_ref = bf16[128,1024]{1,0:T(8,128)(2,1)S(1)} collective-permute-done((bf16[128,1024]{1,0:T(8,128)(2,1)S(1)}, bf16[128,1024]{1,0:T(8,128)(2,1)S(1)}, u32[]{:S(2)}, u32[]{:S(2)}) %collective-permute-start.4) | collective-permute-done | bytes 262176 | tf_op jit(solution)/shard_map/ppermute | solution.py:462
  62.3 2.3 %shard_map.40 = f32[32,8,128]{2,1,0:T(8,128)S(1)} custom-call(s32[4]{0:T(128)S(1)} %pad_add_fusion.ids_ref, f32[8,128]{1,0:T(8,128)S(1)} %get-tuple-element.102.flag_ref, f32[8,1024]{1,0:T(8,128)S(1)} %get-tuple-element.105.rows_ref, f32[1024,128]{1,0:T(8,128)S(1)} %get-tuple-element.106.own_key_ref, f32[16,128]{1,0:T(8,128)S(1)} %get-tuple-element.109.code_ref, ...), custom_call_target="tpu_custom_call" | custom-call | flops 1073741824 | bytes 4194304 | tf_op jit(solution)/shard_map/pallas_call | solution.py:355
  64.6 10.9 %all_to_all.21.in_ref = f32[32,8,128]{2,1,0:T(8,128)S(1)} all-to-all(f32[32,8,128]{2,1,0:T(8,128)S(1)} %shard_map.40), channel_id=1, replica_groups=mesh['x'=4,'core'=2,'yh'=2,'yl'=2,'z'=4] {'core','yh','yl','z'}, dimensions={0} | all-to-all | bytes 262144 | tf_op jit(solution)/shard_map/all_to_all | solution.py:464
  75.5 1.8 %shard_map.41 = (f32[6,128]{1,0:T(8,128)}, s32[1]{0:T(128)}) custom-call(s32[4]{0:T(128)S(1)} %pad_add_fusion.ids_ref, f32[32,8,128]{2,1,0:T(8,128)S(1)} %all_to_all.21.in_ref), custom_call_target="tpu_custom_call" | custom-call | flops 134217728 | bytes 4194304 | tf_op jit(solution)/shard_map/pallas_call | solution.py:355
  77.3 0.8 %while.24 = (s32[]{:T(128)}, f32[768]{0:T(1024)}, bf16[1024,1024]{1,0:T(8,128)(2,1)}, s32[]{:T(128)}, s32[]{:T(128)}, /*index=5*/s32[4]{0:T(128)S(1)}) while((s32[]{:T(128)}, f32[768]{0:T(1024)}, bf16[1024,1024]{1,0:T(8,128)(2,1)}, s32[]{:T(128)}, s32[]{:T(128)}, /*index=5*/s32[4]{0:T(128)S(1)}) %tuple.50), condition=%region_4.5_spmd, body=%region_0.4_spmd | while | flops 2287025152 | bytes 43379448 | solution.py:466
Async XLA Ops:
  44.5 8.8 %collective-permute-start.3 = (bf16[1024,1024]{1,0:T(8,128)(2,1)S(1)}, bf16[1024,1024]{1,0:T(8,128)(2,1)}, u32[]{:S(2)}, u32[]{:S(2)}) collective-permute-start(bf16[1024,1024]{1,0:T(8,128)(2,1)S(1)} %bitcast.27), channel_id=1, source_target_pairs={{0,16},{16,0},{1,17},{17,1},{2,18},{18,2},{3,19},{19,3},{4,20},{20... | collective-permute-start | bytes 6291464 | tf_op jit(solution)/shard_map/ppermute | solution.py:455
  49.8 10.2 %all-to-all-start.2 = ((bf16[8,16,1024]{2,1,0:T(8,128)(2,1)}), bf16[8,16,1024]{2,1,0:T(8,128)(2,1)S(1)}, u32[]{:S(2)}, u32[]{:S(2)}) async-start(bf16[8,16,1024]{2,1,0:T(8,128)(2,1)} %bitcast.6), calls=%async_computation.2 | async-start | bytes 524288 | tf_op jit(solution)/shard_map/all_to_all | solution.py:457
  60.0 2.3 %collective-permute-start.4 = (bf16[128,1024]{1,0:T(8,128)(2,1)S(1)}, bf16[128,1024]{1,0:T(8,128)(2,1)S(1)}, u32[]{:S(2)}, u32[]{:S(2)}) collective-permute-start(bf16[128,1024]{1,0:T(8,128)(2,1)S(1)} %bitcast.32), channel_id=1, source_target_pairs={{0,16},{16,0},{1,17},{17,1},{2,18},{18,2},{3,19},{19,3},{4,20},{20... | collective-permute-start | bytes 786440 | tf_op jit(solution)/shard_map/ppermute | solution.py:462

commit v9 on v7

--- a/solution.py
+++ b/solution.py
@@ -173,14 +173,14 @@
     tag = jnp.where((iota(fixed, 1) & 15) == (iota(fixed, 0) & 15), mm_t(pick, vals), 0.0)
     tag = jnp.broadcast_to(jnp.sum(tag.reshape(LABELS, SLOT, 128), axis=1, keepdims=True), (LABELS, SLOT, 128)).reshape(fixed)
     copies = []
-    for i, b in enumerate(range(0, D, 256)):
-        part = mm(pick, main_ref[:, b:b + 256])
+    for i, b in enumerate(range(0, D, 512)):
+        part = mm(pick, main_ref[:, b:b + 512])
         if b == 0:
             out_ref[:, 0:128] = jnp.where((iota(fixed, 0) & 15) == CAP, tag, part[:, 0:128]).astype(BF)
-            out_ref[:, 128:256] = part[:, 128:256].astype(BF)
+            out_ref[:, 128:512] = part[:, 128:512].astype(BF)
         else:
-            out_ref[:, b:b + 256] = part.astype(BF)
-        copies.append(pltpu.make_async_copy(out_ref.at[:, b:b + 256], out_hbm.at[:, b:b + 256], sems.at[i]))
+            out_ref[:, b:b + 512] = part.astype(BF)
+        copies.append(pltpu.make_async_copy(out_ref.at[:, b:b + 512], out_hbm.at[:, b:b + 512], sems.at[i]))
         copies[-1].start()
     worst = jnp.max(jnp.where(moved, rank, 0.0), axis=1, keepdims=True)
     flag_ref[...] = jnp.broadcast_to(jnp.where(worst >= CAP, 1.0, 0.0), (8, 128))

time: 78.6 us -> 78.6 us (level)
  no operation moved by 1% of the time
where the time goes in v9:
time: 78.6 us; the launch traced here: 78.3 us
  blocking collectives  50.3 us (64%)
  Pallas kernels  16.5 us (21%)
  starting transfers between devices  7.5 us (10%)
  waiting for transfers between devices  2.93 us (4%)
  loops' own time  0.81 us (1%)
    all_to_all x1, blocking collectives, body(): lax.all_to_all(packed.reshape(CHIPS, SLOT, D), CHIP_AXES, split_axis=0, c...  39.5 us
    pallas_call x5, Pallas kernels, call(): pl.pallas_call(kernel, out_shape=shapes, in_specs=specs, out_specs=out_sp...  16.5 us
    all_to_all x1, blocking collectives, body(): back = lax.all_to_all(table, PLANE, split_axis=0, concat_axis=0, tiled=True)  10.9 us
    all_to_all x1, starting transfers between devices, body(): lax.all_to_all(fix.reshape(LABELS, SLOT, D), GROUP_CHIPS, split_axis=0, c...  3.42 us
    ppermute x1, starting transfers between devices, body(): twin = lax.ppermute(main, 'core', swap)  2.94 us
    all_to_all x1, waiting for transfers between devices, body(): lax.all_to_all(fix.reshape(LABELS, SLOT, D), GROUP_CHIPS, split_axis=0, c...  1.77 us
  transfers between devices with their start and end apart: 3, of which 2 were waited for; matrix products, arithmetic and copies ran while one was open for 0% of the time, Pallas kernels for 9%

profile of v9, /device:TPU:1, one launch (start us, length us, event | category | flops | bytes accessed | tf_op | source)
XLA Modules:
  0.0 78.3 jit_solution(3500818878725067885)
XLA Ops:
  0.0 0.1 pad_add_fusion.ids_ref
  0.1 5.0 %shard_map.37 = bf16[1024,1024]{1,0:T(8,128)(2,1)S(1)} custom-call(s32[4]{0:T(128)S(1)} %pad_add_fusion.ids_ref, bf16[768,1024]{1,0:T(8,128)(2,1)} %emb_hbm.1, s32[768]{0:T(1024)} %lab_hbm.1, s32[1,768]{1,0:T(1,128)} %list_hbm.1), custom_call_target="tpu_custom_call" | custom-call | flops 3221225472 | bytes 4194304 | tf_op jit(solution)/shard_map/pallas_call | solution.py:354
  5.1 39.5 %all_to_all.20 = bf16[64,16,1024]{2,1,0:T(8,128)(2,1)S(1)} all-to-all(bf16[64,16,1024]{2,1,0:T(8,128)(2,1)S(1)} %bitcast.31), channel_id=1, replica_groups=mesh['x'=4,'core'=2,'yh'=2,'yl'=2,'z'=4] {'x','yh','yl','z'}, dimensions={0} | all-to-all | bytes 4194304 | tf_op jit(solution)/shard_map/all_to_all | solution.py:450
  44.6 2.9 %collective-permute-start.3 = (bf16[1024,1024]{1,0:T(8,128)(2,1)S(1)}, bf16[1024,1024]{1,0:T(8,128)(2,1)}, u32[]{:S(2)}, u32[]{:S(2)}) collective-permute-start(bf16[1024,1024]{1,0:T(8,128)(2,1)S(1)} %bitcast.27), channel_id=1, source_target_pairs={{0,16},{16,0},{1,17},{17,1},{2,18},{18,2},{3,19},{19,3},{4,20},{20... | collective-permute-start | bytes 6291464 | tf_op jit(solution)/shard_map/ppermute | solution.py:454
  47.5 2.3 %shard_map.38 = (bf16[128,1024]{1,0:T(8,128)(2,1)}, f32[8,128]{1,0:T(8,128)S(1)}, bf16[64,128]{1,0:T(8,128)(2,1)S(1)}, f32[8,1024]{1,0:T(8,128)S(1)}) custom-call(s32[4]{0:T(128)S(1)} %pad_add_fusion.ids_ref, bf16[1024,1024]{1,0:T(8,128)(2,1)S(1)} %bitcast.28), custom_call_target="tpu_custom_call" | custom-call | flops 1073741824 | bytes 4194304 | tf_op jit(solution)/shard_map/pallas_call | solution.py:354
  49.9 3.4 %all-to-all-start.2 = ((bf16[8,16,1024]{2,1,0:T(8,128)(2,1)}), bf16[8,16,1024]{2,1,0:T(8,128)(2,1)S(1)}, u32[]{:S(2)}, u32[]{:S(2)}) async-start(bf16[8,16,1024]{2,1,0:T(8,128)(2,1)} %bitcast.6), calls=%async_computation.2 | async-start | bytes 524288 | tf_op jit(solution)/shard_map/all_to_all | solution.py:456
  53.3 0.0 collective-permute-done.3.twin_hbm
  53.3 4.9 %shard_map.39 = (f32[8,1024]{1,0:T(8,128)S(1)}, f32[1024,128]{1,0:T(8,128)S(1)}, f32[16,128]{1,0:T(8,128)S(1)}) custom-call(s32[4]{0:T(128)S(1)} %pad_add_fusion.ids_ref, bf16[64,128]{1,0:T(8,128)(2,1)S(1)} %get-tuple-element.103.tags_ref, f32[8,1024]{1,0:T(8,128)S(1)} %get-tuple-element.104.lanes_ref, bf16[1024,1024]{1,0:T(8,128)(2,1)S(1)} %bitcast.29, ...), custom_call_target="tpu_custom_call" | custom-call | flops 3221225472 | bytes 4194304 | tf_op jit(solution)/shard_map/pallas_call | solution.py:354
  58.3 1.8 %all-to-all-done.2 = bf16[8,16,1024]{2,1,0:T(8,128)(2,1)S(1)} async-done(((bf16[8,16,1024]{2,1,0:T(8,128)(2,1)}), bf16[8,16,1024]{2,1,0:T(8,128)(2,1)S(1)}, u32[]{:S(2)}, u32[]{:S(2)}) %all-to-all-start.2) | async-done | bytes 262176 | tf_op jit(solution)/shard_map/all_to_all | solution.py:456
  60.0 1.1 %collective-permute-start.4 = (bf16[128,1024]{1,0:T(8,128)(2,1)S(1)}, bf16[128,1024]{1,0:T(8,128)(2,1)S(1)}, u32[]{:S(2)}, u32[]{:S(2)}) collective-permute-start(bf16[128,1024]{1,0:T(8,128)(2,1)S(1)} %bitcast.32), channel_id=1, source_target_pairs={{0,16},{16,0},{1,17},{17,1},{2,18},{18,2},{3,19},{19,3},{4,20},{20... | collective-permute-start | bytes 786440 | tf_op jit(solution)/shard_map/ppermute | solution.py:461
  61.2 1.2 %collective-permute-done.4.fix_twin_ref = bf16[128,1024]{1,0:T(8,128)(2,1)S(1)} collective-permute-done((bf16[128,1024]{1,0:T(8,128)(2,1)S(1)}, bf16[128,1024]{1,0:T(8,128)(2,1)S(1)}, u32[]{:S(2)}, u32[]{:S(2)}) %collective-permute-start.4) | collective-permute-done | bytes 262176 | tf_op jit(solution)/shard_map/ppermute | solution.py:461
  62.3 2.3 %shard_map.40 = f32[32,8,128]{2,1,0:T(8,128)S(1)} custom-call(s32[4]{0:T(128)S(1)} %pad_add_fusion.ids_ref, f32[8,128]{1,0:T(8,128)S(1)} %get-tuple-element.102.flag_ref, f32[8,1024]{1,0:T(8,128)S(1)} %get-tuple-element.105.rows_ref, f32[1024,128]{1,0:T(8,128)S(1)} %get-tuple-element.106.own_key_ref, f32[16,128]{1,0:T(8,128)S(1)} %get-tuple-element.109.code_ref, ...), custom_call_target="tpu_custom_call" | custom-call | flops 1073741824 | bytes 4194304 | tf_op jit(solution)/shard_map/pallas_call | solution.py:354
  64.7 10.9 %all_to_all.21.in_ref = f32[32,8,128]{2,1,0:T(8,128)S(1)} all-to-all(f32[32,8,128]{2,1,0:T(8,128)S(1)} %shard_map.40), channel_id=1, replica_groups=mesh['x'=4,'core'=2,'yh'=2,'yl'=2,'z'=4] {'core','yh','yl','z'}, dimensions={0} | all-to-all | bytes 262144 | tf_op jit(solution)/shard_map/all_to_all | solution.py:463
  75.5 1.8 %shard_map.41 = (f32[6,128]{1,0:T(8,128)}, s32[1]{0:T(128)}) custom-call(s32[4]{0:T(128)S(1)} %pad_add_fusion.ids_ref, f32[32,8,128]{2,1,0:T(8,128)S(1)} %all_to_all.21.in_ref), custom_call_target="tpu_custom_call" | custom-call | flops 134217728 | bytes 4194304 | tf_op jit(solution)/shard_map/pallas_call | solution.py:354
  77.4 0.8 %while.24 = (s32[]{:T(128)}, f32[768]{0:T(1024)}, bf16[1024,1024]{1,0:T(8,128)(2,1)}, s32[]{:T(128)}, s32[]{:T(128)}, /*index=5*/s32[4]{0:T(128)S(1)}) while((s32[]{:T(128)}, f32[768]{0:T(1024)}, bf16[1024,1024]{1,0:T(8,128)(2,1)}, s32[]{:T(128)}, s32[]{:T(128)}, /*index=5*/s32[4]{0:T(128)S(1)}) %tuple.50), condition=%region_4.5_spmd, body=%region_0.4_spmd | while | flops 2287025152 | bytes 43379448 | solution.py:465
Async XLA Ops:
  44.6 8.7 %collective-permute-start.3 = (bf16[1024,1024]{1,0:T(8,128)(2,1)S(1)}, bf16[1024,1024]{1,0:T(8,128)(2,1)}, u32[]{:S(2)}, u32[]{:S(2)}) collective-permute-start(bf16[1024,1024]{1,0:T(8,128)(2,1)S(1)} %bitcast.27), channel_id=1, source_target_pairs={{0,16},{16,0},{1,17},{17,1},{2,18},{18,2},{3,19},{19,3},{4,20},{20... | collective-permute-start | bytes 6291464 | tf_op jit(solution)/shard_map/ppermute | solution.py:454
  49.9 10.2 %all-to-all-start.2 = ((bf16[8,16,1024]{2,1,0:T(8,128)(2,1)}), bf16[8,16,1024]{2,1,0:T(8,128)(2,1)S(1)}, u32[]{:S(2)}, u32[]{:S(2)}) async-start(bf16[8,16,1024]{2,1,0:T(8,128)(2,1)} %bitcast.6), calls=%async_computation.2 | async-start | bytes 524288 | tf_op jit(solution)/shard_map/all_to_all | solution.py:456
  60.0 2.3 %collective-permute-start.4 = (bf16[128,1024]{1,0:T(8,128)(2,1)S(1)}, bf16[128,1024]{1,0:T(8,128)(2,1)S(1)}, u32[]{:S(2)}, u32[]{:S(2)}) collective-permute-start(bf16[128,1024]{1,0:T(8,128)(2,1)S(1)} %bitcast.32), channel_id=1, source_target_pairs={{0,16},{16,0},{1,17},{17,1},{2,18},{18,2},{3,19},{19,3},{4,20},{20... | collective-permute-start | bytes 786440 | tf_op jit(solution)/shard_map/ppermute | solution.py:461
